TPU v7x, 128 devices: a whole 4x4x4 slice. The times are simulated.
128 devices in a mesh: dp: 8 (over y_hi, z), owner: 16 (over y_lo, x, core).
Axes of the slice: x: 4, y: 4 (y_hi: 2, y_lo: 2; y = y_hi * 2 + y_lo), z: 4, core: 2. Of those that a mesh axis runs over, the one named last changes fastest.
Arguments:
- activations: bfloat16 [6144, 6144], P('dp', 'owner'), may hold values from -6 to 6
- out_grads: bfloat16 [6144, 6144], P('dp'), may hold values from -0.078125 to 0.078125
- basis_in: bfloat16 [6144, 6144], P('owner'), may hold values from -0.078125 to 0.078125
- basis_out: bfloat16 [6144, 6144], P(None, 'owner'), may hold values from -0.078125 to 0.078125
- eig_in: float32 [6144], replicated, may hold values from 0.3 to 3
- eig_out: float32 [6144], replicated, may hold values from 0.3 to 3
Outputs:
- precond: bfloat16 [6144, 6144], P(None, 'owner')
All inputs are finite; a program needn't handle non-finite values.
Results may differ from a plain program's by a relative error of at most 0.03.
Values may be sent and summed in bfloat16 or wider, within the bound.
A program may use at most 128 MiB of HBM per device.

v0:
```python
import jax
import jax.numpy as jnp
from jax import lax
from jax.sharding import PartitionSpec as P

damping = 0.1


def shards(activations, out_grads, basis_in, basis_out, eig_in, eig_out):
    rep_count = lax.axis_size("dp")
    own_count = lax.axis_size("owner")
    rep_index = lax.axis_index("dp")
    own_index = lax.axis_index("owner")
    own_rows = basis_in.shape[0]
    own_cols = basis_out.shape[1]
    slab_rows = own_rows // rep_count
    grad_cols = lax.psum_scatter(
        lax.dot_general(
            out_grads, activations, (((0,), (0,)), ((), ())), preferred_element_type=jnp.float32
        ).astype(jnp.bfloat16),
        "dp",
        scatter_dimension=0,
        tiled=True,
    )
    basis_part = basis_in
    rotated = lax.dot_general(
        basis_part,
        lax.all_gather(grad_cols, "owner", axis=1, tiled=True),
        (((1,), (1,)), ((), ())),
        preferred_element_type=jnp.float32,
    ).astype(jnp.bfloat16)
    left_slabs = lax.all_to_all(rotated, "dp", split_axis=0, concat_axis=1, tiled=True)
    product = jnp.dot(
        lax.all_gather(left_slabs, "owner", axis=0, tiled=True),
        basis_out,
        preferred_element_type=jnp.float32,
    )
    eig_rows = lax.dynamic_slice_in_dim(
        eig_in.reshape(own_count, rep_count, slab_rows), rep_index, 1, 1
    ).reshape(own_count * slab_rows)
    eig_cols = lax.dynamic_slice_in_dim(eig_out, own_index * own_cols, own_cols, 0)
    scaled = (product / (eig_rows[:, None] * eig_cols[None, :] + damping)).astype(jnp.bfloat16)
    basis_part = basis_out
    back_sum = lax.psum_scatter(
        lax.dot_general(
            basis_part, scaled, (((1,), (1,)), ((), ())), preferred_element_type=jnp.float32
        ).astype(jnp.bfloat16),
        "owner",
        scatter_dimension=0,
        tiled=True,
    )
    own_slab = lax.dynamic_slice_in_dim(basis_in, rep_index * slab_rows, slab_rows, 0)
    summand = lax.dot_general(
        lax.all_gather(own_slab, "owner", axis=0, tiled=True),
        back_sum,
        (((0,), (1,)), ((), ())),
        preferred_element_type=jnp.float32,
    )
    result = lax.psum(summand.astype(jnp.bfloat16), "dp")
    return result


def solution(mesh):
    in_specs = (P("dp", "owner"), P("dp", None), P("owner", None), P(None, "owner"), P(), P())
    out_specs = P(None, "owner")
    return jax.shard_map(shards, mesh=mesh, in_specs=in_specs, out_specs=out_specs, check_vma=False)
```

profile of v0, /device:TPU:1, one launch (start us, length us, event | category | flops | bytes accessed | tf_op | source)
XLA Modules:
  0.0 525.7 jit_solution(1953350666802447125)
XLA Ops:
  6.5 0.0 copy-start
  6.5 0.0 reduce-scatter.5.cloned.1.call-start
  6.5 1.1 copy-done
  7.6 9.1 %convolution_convert_fusion.2 = bf16[6144,384]{1,0:T(8,128)(2,1)} fusion(bf16[768,6144]{1,0:T(8,128)(2,1)} %param.7, bf16[768,384]{1,0:T(8,128)(2,1)S(1)} %copy-done), kind=kOutput, calls=%fused_computation.3 | convolution fusion | flops 3626237952 | bytes 14745600 | tf_op jit(solution)/shard_map/dot_general | solution.py:18
  16.7 0.0 reduce-scatter.5.cloned.1.call-update
  16.7 0.0 all-gather.6.cloned.1.call-start
  16.7 90.3 %reduce-scatter.5.cloned.1.call-done = bf16[768,384]{1,0:T(8,128)(2,1)} async-done(((bf16[6144,384]{1,0:T(8,128)(2,1)}), bf16[768,384]{1,0:T(8,128)(2,1)}) %reduce-scatter.5.cloned.1.call-update) | async-done | bytes 589840 | tf_op jit(solution)/shard_map/reduce_scatter | solution.py:17
  107.0 0.0 all-gather.6.cloned.1.call-update
  107.0 0.0 all-gather.8.cloned.1.call-start
  107.1 58.8 %all-gather.6.cloned.1.call-done = bf16[768,6144]{1,0:T(8,128)(2,1)} async-done(((bf16[768,384]{1,0:T(8,128)(2,1)}), bf16[768,6144]{1,0:T(8,128)(2,1)}) %all-gather.6.cloned.1.call-update) | async-done | bytes 9437200 | tf_op jit(solution)/shard_map/all_gather | solution.py:28
  165.9 8.9 %convolution_convert_fusion.3 = bf16[768,384]{0,1:T(8,128)(2,1)S(1)} fusion(bf16[768,6144]{1,0:T(8,128)(2,1)} %all-gather.6.cloned.1.call-done, bf16[384,6144]{1,0:T(8,128)(2,1)} %param.8), kind=kOutput, calls=%fused_computation.4 | convolution fusion | flops 3624173568 | bytes 14745600 | tf_op jit(solution)/shard_map/dot_general | solution.py:26
  174.8 0.0 copy-start.2
  174.8 18.1 %all_to_all.19 = bf16[8,48,768]{2,1,0:T(8,128)(2,1)S(1)} all-to-all(bf16[8,48,768]{2,1,0:T(8,128)(2,1)S(1)} %bitcast.21), channel_id=1, replica_groups=mesh['dp'=8,'owner'=16] {'dp'}, dimensions={0} | all-to-all | bytes 1179648 | tf_op jit(solution)/shard_map/all_to_all | solution.py:32
  192.9 0.9 copy.11
  193.7 0.0 all-gather.8.cloned.1.call-update
  193.8 0.0 all-gather.4.cloned.1.call-start
  193.8 1.9 constant_dynamic-slice_fusion
  195.7 0.0 all-gather.4.cloned.1.call-update
  195.8 0.0 reduce-scatter.7.cloned.1.call-start
  195.8 0.0 copy-done.2
  195.8 0.1 reshape.8
  196.0 0.1 mul.22
  196.0 0.8 dynamic_slice.11
  196.8 52.2 %all-gather.8.cloned.1.call-done = bf16[768,6144]{1,0:T(8,128)(2,1)} async-done(((bf16[48,6144]{1,0:T(8,128)(2,1)}), bf16[768,6144]{1,0:T(8,128)(2,1)}) %all-gather.8.cloned.1.call-update) | async-done | bytes 9437200 | tf_op jit(solution)/shard_map/all_gather | solution.py:34
  249.0 9.0 %fusion.1 = bf16[768,384]{1,0:T(8,128)(2,1)S(1)} fusion(bf16[768,6144]{1,0:T(8,128)(2,1)} %all-gather.8.cloned.1.call-done, bf16[6144,384]{1,0:T(8,128)(2,1)} %param.9, f32[384]{0:T(512)S(1)} %dynamic_slice.11, f32[768]{0:T(1024)S(1)} %mul.22), kind=kOutput, calls=%fused_computation.6 | convolution fusion | flops 3625058304 | bytes 14750208 | tf_op jit(solution)/shard_map/dot_general | solution.py:33
  258.0 9.9 %fusion = bf16[6144,768]{0,1:T(8,128)(2,1)} fusion(bf16[768,384]{1,0:T(8,128)(2,1)S(1)} %fusion.1, bf16[6144,384]{1,0:T(8,128)(2,1)} %param.9), kind=kOutput, calls=%fused_computation.1 | convolution fusion | flops 3628597248 | bytes 14745600 | tf_op jit(solution)/shard_map/dot_general | solution.py:45
  267.9 12.8 %copy.9 = bf16[6144,768]{1,0:T(8,128)(2,1)} copy(bf16[6144,768]{0,1:T(8,128)(2,1)} %fusion) | data formatting | bytes 18874368
  280.7 0.0 reduce-scatter.7.cloned.1.call-update
  280.7 0.2 all-reduce.2.cloned.1.call-start
  280.9 27.6 %all-gather.4.cloned.1.call-done = bf16[768,6144]{1,0:T(8,128)(2,1)} async-done(((bf16[48,6144]{1,0:T(8,128)(2,1)}), bf16[768,6144]{1,0:T(8,128)(2,1)}) %all-gather.4.cloned.1.call-update) | async-done | bytes 9437200 | tf_op jit(solution)/shard_map/all_gather | solution.py:54
  308.5 75.6 %reduce-scatter.7.cloned.1.call-done = bf16[384,768]{1,0:T(8,128)(2,1)} async-done(((bf16[6144,768]{1,0:T(8,128)(2,1)}), bf16[384,768]{1,0:T(8,128)(2,1)}) %reduce-scatter.7.cloned.1.call-update) | async-done | bytes 589840
  384.1 9.2 %convolution_convert_fusion.1 = bf16[6144,384]{1,0:T(8,128)(2,1)} fusion(bf16[768,6144]{1,0:T(8,128)(2,1)} %all-gather.4.cloned.1.call-done, bf16[384,768]{1,0:T(8,128)(2,1)} %reduce-scatter.7.cloned.1.call-done), kind=kOutput, calls=%fused_computation.2 | convolution fusion | flops 3626237952 | bytes 14745600 | tf_op jit(solution)/shard_map/dot_general | solution.py:53
  393.4 0.0 all-reduce.2.cloned.1.call-update
  393.4 0.0 copy-start.1
  393.4 120.5 %all-reduce.2.cloned.1.call-done = bf16[6144,384]{1,0:T(8,128)(2,1)} async-done(((bf16[6144,384]{1,0:T(8,128)(2,1)}), bf16[6144,384]{1,0:T(8,128)(2,1)}) %all-reduce.2.cloned.1.call-update) | async-done | bytes 4718608 | tf_op jit(solution)/shard_map/psum | solution.py:59
  513.9 5.0 copy.13
  518.9 0.0 copy-done.1
  (1 shorter events, 0.0 us)
Async XLA Ops:
  6.5 1.1 copy-start
  6.5 100.5 %reduce-scatter.5.cloned.1.call-start = ((), (), s32[]{:S(2)}) async-start(), calls=%async_computation.4 | async-start | bytes 5308416 | tf_op jit(solution)/shard_map/reduce_scatter | solution.py:17
  16.7 149.2 %all-gather.6.cloned.1.call-start = ((), (), s32[]{:S(2)}) async-start(), calls=%async_computation.5 | async-start | bytes 10027008 | tf_op jit(solution)/shard_map/all_gather | solution.py:28
  107.0 141.9 %all-gather.8.cloned.1.call-start = ((), (), s32[]{:S(2)}) async-start(), calls=%async_computation.6 | async-start | bytes 10027008 | tf_op jit(solution)/shard_map/all_gather | solution.py:34
  174.8 21.0 %copy-start.2 = (f32[6144]{0:T(1024)S(1)}, f32[6144]{0:T(1024)}, u32[]{:S(2)}) copy-start(f32[6144]{0:T(1024)} %param.10) | copy-start | bytes 73732
  193.8 114.7 %all-gather.4.cloned.1.call-start = ((), (), s32[]{:S(2)}) async-start(), calls=%async_computation.3 | async-start | bytes 10027008 | tf_op jit(solution)/shard_map/all_gather | solution.py:54
  195.8 188.4 %reduce-scatter.7.cloned.1.call-start = ((), (), s32[]{:S(2)}) async-start(), calls=%async_computation.8 | async-start | bytes 10027008
  280.7 233.2 %all-reduce.2.cloned.1.call-start = ((), (), s32[]{:S(2)}) async-start(), calls=%async_computation.7 | async-start | bytes 9437184 | tf_op jit(solution)/shard_map/psum | solution.py:59
  393.4 125.5 %copy-start.1 = (bf16[768,384]{1,0:T(8,128)(2,1)S(1)}, bf16[768,384]{1,0:T(8,128)(2,1)}, u32[]{:S(2)}) copy-start(bf16[768,384]{1,0:T(8,128)(2,1)} %param.6) | copy-start | bytes 1769476
Sparse Core Ops, SparseCore 0:
  16.8 90.1 reduce-scatter.4
  108.7 57.1 all-gather.5
  193.9 55.0 all-gather.7
  250.5 57.8 all-gather.3
  310.7 73.3 reduce-scatter.6
  393.5 120.2 all-reduce.1
where the time goes:
time: 526 us
  waiting for transfers between devices  425 us (81%)
  matrix products  46.1 us (9%)
  local copies, waits for them, and re-layouts  22.6 us (4%)
  blocking collectives  18.1 us (3%)
  between operations  13.5 us (3%)
    psum x1, waiting for transfers between devices, shards(): result = lax.psum(summand.astype(jnp.bfloat16), 'dp')  120 us
    reduce_scatter x1, waiting for transfers between devices, shards(): lax.psum_scatter(lax.dot_general(out_grads, activations, (((0,), (0,)), (...  90.3 us
    unnamed x7, waiting for transfers between devices  75.7 us
    all_gather x1, waiting for transfers between devices, shards(): lax.all_gather(grad_cols, 'owner', axis=1, tiled=True)  58.8 us
    all_gather x1, waiting for transfers between devices, shards(): lax.all_gather(left_slabs, 'owner', axis=0, tiled=True)  52.2 us
    all_gather x1, waiting for transfers between devices, shards(): lax.all_gather(own_slab, 'owner', axis=0, tiled=True)  27.6 us
    unnamed x8, local copies, waits for them, and re-layouts  18.9 us
    all_to_all x1, blocking collectives, shards(): lax.all_to_all(rotated, 'dp', split_axis=0, concat_axis=1, tiled=True)  18.1 us
  transfers between devices with their start and end apart: 6, of which 6 were waited for; matrix products, arithmetic and copies ran while one was open for 7% of the time, Pallas kernels for 0%

commit v1 on v0

v1 whole, which is shorter than its diff:
```python
import jax
import jax.numpy as jnp
from jax import lax
from jax.experimental import pallas as pl
from jax.experimental.pallas import tpu as pltpu
from jax.sharding import PartitionSpec as P

damping = 0.1
bf16 = jnp.bfloat16
f32 = jnp.float32
MESH = pl.DeviceIdType.MESH


def device(yh, z, yl, x, c):
    return (yh * 4 + z, yl * 8 + x * 2 + c)


def visit(s, p, q):
    k = s % 3
    last = s // 6
    dq = (1 - last) * (k * (k + 1) // 2) + 2 * last
    dp = (1 - last) * (s // 3) + last * k
    return (p + dp) % 2, (q + dq) % 4


class Gather:
    def __init__(self, part, ssem, rsem, p, q, to):
        self.part, self.ssem, self.rsem, self.p, self.q, self.to = part, ssem, rsem, p, q, to

    def copy(self, k):
        p, q = self.p, self.q
        o, r, l = 1 - p, (q + 1) % 4, (q + 3) % 4
        pp, qq, half, dest = (
            (p, q, None, (o, q)),
            (p, q, None, (p, r)),
            (p, q, None, (p, l)),
            (o, q, None, (p, r)),
            (o, q, None, (p, l)),
            (p, l, 0, (p, r)),
            (p, r, 1, (p, l)),
            (o, l, 0, (p, r)),
            (o, r, 1, (p, l)),
        )[k]
        ref = self.part(pp * 4 + qq, half)
        return pltpu.make_async_remote_copy(
            ref, ref, self.ssem.at[k], self.rsem.at[k], device_id=self.to(*dest), device_id_type=MESH
        )

    def start(self, *ks):
        for k in ks:
            self.copy(k).start()

    def got(self, *ks):
        p, q = self.p, self.q
        o, r, l, a = 1 - p, (q + 1) % 4, (q + 3) % 4, (q + 2) % 4
        for k in ks:
            pp, qq, half = (
                (o, q, None), (p, l, None), (p, r, None), (o, l, None), (o, r, None),
                (p, a, 0), (p, a, 1), (o, a, 0), (o, a, 1),
            )[k]
            ref = self.part(pp * 4 + qq, half)
            pltpu.make_async_remote_copy(
                ref, ref, self.ssem.at[k], self.rsem.at[k], device_id=self.to(o, q), device_id_type=MESH
            ).wait_recv()

    def first(self):
        self.start(0, 1, 2)

    def second(self):
        self.got(0)
        self.start(3, 4)
        self.got(1)
        self.start(5)
        self.got(2)
        self.start(6)

    def third(self):
        self.got(3)
        self.start(7)
        self.got(4)
        self.start(8)

    def sent(self):
        for k in range(9):
            self.copy(k).wait_send()


def kernel(
    at_ref, g_ref, bi_ref, bo_ref, ein_ref, eout_ref, o_ref,
    ag, ym, zp, zbuf, zsend, zy, zfull, big, pp, pbuf, psend, py, sc, bo,
    wbuf, wsend, wy, wg, acc, frecv,
    lsem, gsem, bsem, tsem, osem,
    a_s, a_r, b_s, b_r, w_s, w_r, o_s, o_r,
    z_s, z_r, zy_s, zy_r, p_s, p_r, py_s, py_r, x_s, x_r, xy_s, xy_r, sib_s, sib_r,
):
    rep = lax.axis_index("dp")
    own = lax.axis_index("owner")
    yh, z = rep // 4, rep % 4
    yl, x, c = own // 8, (own // 2) % 4, own % 2
    m = yl * 4 + x
    oc = 1 - c

    def remote(src, dst, s, r, dest):
        return pltpu.make_async_remote_copy(src, dst, s, r, device_id=dest, device_id_type=MESH)

    sibling = device(yh, z, yl, x, oc)
    ypair = device(1 - yh, z, yl, x, c)
    lpair = device(yh, z, 1 - yl, x, c)
    over_owner = lambda p, q: device(yh, z, p, q, c)
    over_dp = lambda p, q: device(p, q, yl, x, c)

    barrier = pltpu.get_barrier_semaphore()
    partners = [sibling, ypair, lpair]
    partners += [over_owner(yl, (x + d) % 4) for d in (1, 2, 3)]
    partners += [over_dp(yh, (z + d) % 4) for d in (1, 2, 3)]
    for dest in partners:
        pl.semaphore_signal(barrier, inc=1, device_id=dest, device_id_type=MESH)

    def bo_chunk(k):
        rows = pl.ds(pl.multiple_of(k * 768, 768), 768)
        return pltpu.make_async_copy(bo_ref.at[rows], bo.at[c, rows], bsem.at[k])

    def g_half(k, h):
        cols = pl.ds(pl.multiple_of(k * 768, 768), 768)
        return pltpu.make_async_copy(
            g_ref.at[pl.ds(h * 384, 384), cols], zp.at[2 * (k % 4) + h], gsem.at[k % 4, h]
        )

    def tile_start(q, core):
        return pl.multiple_of(((2 * (q // 3) + core) * 3 + q % 3) * 128, 128)

    def bi_tile(j):
        dst = big.at[m, :, :, pl.ds(j * 128, 128)]
        return pltpu.make_async_copy(
            bi_ref.at[:, :, pl.ds(tile_start(rep + 8 * (j % 3), j // 3), 128)], dst, tsem.at[j]
        )

    load_a = pltpu.make_async_copy(at_ref, ag.at[m], lsem.at[0])
    load_a.start()
    for k in range(8):
        bo_chunk(k).start()
        if k < 4:
            g_half(k, 0).start()
            g_half(k, 1).start()
    for j in range(6):
        bi_tile(j).start()

    gather_a = Gather(
        lambda slot, h: ag.at[slot] if h is None else ag.at[slot, pl.ds(h * 192, 192)],
        a_s, a_r, yl, x, over_owner,
    )
    gather_b = Gather(
        lambda slot, h: big.at[slot] if h is None else big.at[slot, pl.ds(h * 4, 4)],
        b_s, b_r, yl, x, over_owner,
    )
    gather_w = Gather(
        lambda slot, h: wg.at[slot] if h is None else wg.at[slot, pl.ds(h * 192, 192)],
        w_s, w_r, yh, z, over_dp,
    )
    gather_o = Gather(
        lambda slot, h: ag.at[slot] if h is None else ag.at[slot, pl.ds(h * 192, 192)],
        o_s, o_r, yh, z, over_dp,
    )

    load_a.wait()
    pl.semaphore_wait(barrier, len(partners))
    gather_a.first()
    send_bo = remote(bo_ref, bo.at[c], sib_s.at[0], sib_r.at[0], sibling)
    send_bo.start()

    half = pl.ds(0, 384)
    acc[:, half] = jnp.zeros((768, 384), f32)

    @pl.loop(0, 8)
    def _(k):
        bo_chunk(k).wait()
        g_half(k, 0).wait()
        g_half(k, 1).wait()
        rows = pl.ds(pl.multiple_of(k * 768, 768), 768)
        part = zp[pl.ds(2 * (k % 4), 2)].reshape(768, 768)
        acc[:, half] += jnp.dot(part, bo[c, rows, :], preferred_element_type=f32)

        @pl.when(k < 4)
        def _():
            g_half(k + 4, 0).start()
            g_half(k + 4, 1).start()

    mine = pl.ds(pl.multiple_of(c * 384, 128), 384)
    other = pl.ds(pl.multiple_of(oc * 384, 128), 384)
    ym[:, mine] = acc[:, half].astype(bf16)
    send_y = remote(ym.at[:, mine], ym.at[:, mine], sib_s.at[1], sib_r.at[1], sibling)
    send_y.start()
    remote(ym.at[:, other], ym.at[:, other], sib_s.at[1], sib_r.at[1], sibling).wait_recv()

    def z_part(q):
        return zp.at[q // 3, pl.ds(pl.multiple_of((q % 3) * 128, 128), 128)]

    def z_copy(yt, i, dz):
        zt = (z + dz) % 4
        j = yt * 3 + i
        return remote(
            z_part(yt * 4 + zt + 8 * i), zbuf.at[dz - 1, j], z_s.at[dz - 1, j], z_r.at[dz - 1, j], over_dp(yh, zt)
        )

    @pl.loop(0, 8)
    def _(s):
        @pl.when(s == 1)
        def _():
            gather_a.second()

        @pl.when(s == 4)
        def _():
            gather_a.third()

        @pl.when(s == 6)
        def _():
            gather_a.got(5, 6)
            for j in range(6):
                bi_tile(j).wait()
            gather_b.first()

        @pl.when(s == 7)
        def _():
            gather_a.got(7, 8)

        p_, q_ = visit(s, yl, x)
        blk = p_ * 4 + q_
        zp[blk] = jnp.dot(ag[blk], ym[...], preferred_element_type=f32).astype(bf16)

        @pl.loop(0, 3)
        def _(t):
            q = 3 * blk + t
            r_, i = q % 8, q // 8
            dz = (r_ % 4 + 4 - z) % 4

            @pl.when(dz != 0)
            def _():
                z_copy(r_ // 4, i, dz).start()

    gather_a.sent()
    gather_b.second()

    def z_sum(yt, i):
        j = yt * 3 + i
        total = z_part(yt * 4 + z + 8 * i)[...].astype(f32)
        for d in range(3):
            remote(zbuf.at[d, j], zbuf.at[d, j], z_s.at[d, j], z_r.at[d, j], ypair).wait_recv()
            total = total + zbuf[d, j].astype(f32)
        return total

    def zy_copy(i):
        return remote(zsend.at[i], zy.at[i], zy_s.at[i], zy_r.at[i], ypair)

    @pl.loop(0, 3)
    def _(i):
        zsend[i] = z_sum(1 - yh, i).astype(bf16)
        zy_copy(i).start()

    def z_rows(core):
        return zfull.at[pl.ds(pl.multiple_of(core * 384, 128), 384)]

    @pl.loop(0, 3)
    def _(i):
        total = z_sum(yh, i)
        zy_copy(i).wait()
        total = total + zy[i].astype(f32)
        zfull[pl.ds(pl.multiple_of(c * 384 + i * 128, 128), 128), :] = total.astype(bf16)

    send_z = remote(z_rows(c), z_rows(c), sib_s.at[2], sib_r.at[2], sibling)
    send_z.start()
    gather_b.third()
    remote(z_rows(oc), z_rows(oc), sib_s.at[2], sib_r.at[2], sibling).wait_recv()

    def p_copy(blk, dz):
        zt = (z + dz) % 4
        return remote(
            pp.at[blk, pl.ds(zt * 2, 2)], pbuf.at[dz - 1, blk], p_s.at[dz - 1, blk], p_r.at[dz - 1, blk],
            over_dp(yh, zt),
        )

    @pl.loop(0, 8)
    def _(s):
        @pl.when(s == 6)
        def _():
            gather_b.got(5, 6)

        @pl.when(s == 7)
        def _():
            gather_b.got(7, 8)

        p_, q_ = visit(s, yl, x)
        blk = p_ * 4 + q_
        part = jnp.dot(big[blk].reshape(384, 768), zfull[...], preferred_element_type=f32)
        pp[blk] = part.astype(bf16).reshape(8, 48, 768)
        for dz in (1, 2, 3):
            p_copy(blk, dz).start()

    gather_b.sent()

    @pl.loop(0, 6)
    def _(j):
        for dz in (1, 2, 3):
            z_copy(j // 3, j % 3, dz).wait_send()

    def p_sum(blk, h):
        total = pp[blk, 2 * z + h].astype(f32)
        for d in range(3):
            total = total + pbuf[d, blk, h].astype(f32)
        return total

    def py_copy(blk):
        return remote(psend.at[blk], py.at[blk], py_s.at[blk], py_r.at[blk], ypair)

    @pl.loop(0, 8)
    def _(s):
        p_, q_ = visit(s, yl, x)
        blk = p_ * 4 + q_
        for d in range(3):
            remote(pbuf.at[d, blk], pbuf.at[d, blk], p_s.at[d, blk], p_r.at[d, blk], ypair).wait_recv()
        psend[blk] = p_sum(blk, 1 - yh).astype(bf16)
        py_copy(blk).start()

    @pl.loop(0, 8)
    def _(s):
        p_, q_ = visit(s, yl, x)
        blk = p_ * 4 + q_
        py_copy(blk).wait()
        total = p_sum(blk, yh) + py[blk].astype(f32)
        scale = ein_ref[blk] * eout_ref[pl.ds(m, 1), :] + damping
        sc[blk] = (total / scale).astype(bf16)
        for dz in (1, 2, 3):
            p_copy(blk, dz).wait_send()

    remote(bo_ref, bo.at[oc], sib_s.at[0], sib_r.at[0], sibling).wait_recv()
    nt = (((1,), (1,)), ((), ()))

    def w_copy(dx, yt):
        xt = (x + dx) % 4
        j = (dx - 1) * 2 + yt
        return remote(zp.at[yt * 4 + xt], wbuf.at[j], x_s.at[j], x_r.at[j], over_owner(yl, xt))

    @pl.loop(0, 8)
    def _(s):
        dx, yt = (s // 2 + 1) % 4, s % 2
        blk = yt * 4 + (x + dx) % 4
        rows = pl.ds(pl.multiple_of(blk * 768, 768), 768)
        lhs = sc[...].reshape(384, 768)
        part = lax.dot_general(lhs[:, :384], bo[0, rows, :], nt, preferred_element_type=f32)
        part += lax.dot_general(lhs[:, 384:], bo[1, rows, :], nt, preferred_element_type=f32)
        zp[blk] = part.astype(bf16)

        @pl.when(dx != 0)
        def _():
            w_copy(dx, yt).start()

    def w_got(yt):
        for d in range(3):
            j = d * 2 + yt
            remote(wbuf.at[j], wbuf.at[j], x_s.at[j], x_r.at[j], lpair).wait_recv()

    def w_sum(yt, rows):
        total = zp[yt * 4 + x, rows].astype(f32)
        for d in range(3):
            total = total + wbuf[d * 2 + yt, rows].astype(f32)
        return total

    def wy_copy(i):
        return remote(wsend.at[i], wy.at[i], xy_s.at[i], xy_r.at[i], lpair)

    w_got(1 - yl)

    @pl.loop(0, 3)
    def _(i):
        wsend[i] = w_sum(1 - yl, pl.ds(pl.multiple_of(i * 128, 128), 128)).astype(bf16)
        wy_copy(i).start()

    w_got(yl)

    @pl.loop(0, 3)
    def _(i):
        rows = pl.ds(pl.multiple_of(i * 128, 128), 128)
        total = w_sum(yl, rows)
        wy_copy(i).wait()
        wg[rep, rows] = (total + wy[i].astype(f32)).astype(bf16)

    @pl.loop(0, 3)
    def _(d):
        for yt in range(2):
            w_copy(d + 1, yt).wait_send()

    gather_w.first()
    acc[...] = jnp.zeros_like(acc)

    @pl.loop(0, 8)
    def _(s):
        @pl.when(s == 1)
        def _():
            gather_w.second()

        @pl.when(s == 4)
        def _():
            gather_w.third()

        @pl.when(s == 6)
        def _():
            gather_w.got(5, 6)

        @pl.when(s == 7)
        def _():
            gather_w.got(7, 8)

        p_, q_ = visit(s, yh, z)
        lhs = big[:, q_ * 2 + p_].reshape(384, 768)
        acc[...] += lax.dot_general(
            lhs, wg[p_ * 4 + q_], (((0,), (0,)), ((), ())), preferred_element_type=f32
        )

    gather_w.sent()
    send_f = remote(acc.at[:, other], frecv, sib_s.at[3], sib_r.at[3], sibling)
    send_f.start()
    remote(frecv, frecv, sib_s.at[3], sib_r.at[3], sibling).wait_recv()
    for core in range(2):
        rows = pl.ds(core * 384, 384)
        ag[rep, :, pl.ds(core * 384, 384)] = (acc[rows, mine] + frecv[rows, :]).astype(bf16)

    gather_o.first()

    def store(r_, j):
        src = ag.at[r_, pl.ds((j % 3) * 128, 128), pl.ds((j // 3) * 384, 384)]
        dst = o_ref.at[pl.ds(tile_start(r_ + 8 * (j % 3), j // 3), 128)]
        return pltpu.make_async_copy(src, dst, osem.at[r_, j])

    @pl.loop(0, 8)
    def _(s):
        @pl.when(s == 1)
        def _():
            gather_o.second()

        @pl.when(s == 4)
        def _():
            gather_o.third()

        @pl.when(s == 6)
        def _():
            gather_o.got(5, 6)

        @pl.when(s == 7)
        def _():
            gather_o.got(7, 8)

        p_, q_ = visit(s, yh, z)
        for j in range(6):
            store(p_ * 4 + q_, j).start()

    gather_o.sent()
    send_bo.wait_send()
    send_y.wait_send()
    send_z.wait_send()
    send_f.wait_send()

    @pl.loop(0, 8)
    def _(r_):
        for j in range(6):
            store(r_, j).wait()


def shards(activations, out_grads, basis_in, basis_out, eig_in, eig_out):
    rep = lax.axis_index("dp")
    core = lax.axis_index("owner") % 2
    sub = (rep % 4) * 2 + rep // 4
    ein = lax.dynamic_slice(eig_in.reshape(8, 2, 8, 48), (0, core, sub, 0), (8, 1, 1, 48)).reshape(8, 48, 1)
    dma = pltpu.SemaphoreType.DMA
    v = pltpu.VMEM
    scratch = [
        v((8, 384, 768), bf16), v((768, 768), bf16), v((8, 384, 768), bf16), v((3, 6, 128, 768), bf16),
        v((3, 128, 768), bf16), v((3, 128, 768), bf16), v((768, 768), bf16), v((8, 8, 48, 768), bf16),
        v((8, 8, 48, 768), bf16), v((3, 8, 2, 48, 768), bf16), v((8, 48, 768), bf16), v((8, 48, 768), bf16),
        v((8, 48, 768), bf16), v((2, 6144, 384), bf16),
        v((6, 384, 768), bf16), v((3, 128, 768), bf16), v((3, 128, 768), bf16), v((8, 384, 768), bf16),
        v((768, 768), f32), v((768, 384), f32),
        dma((1,)), dma((4, 2)), dma((8,)), dma((6,)), dma((8, 6)),
    ]
    scratch += [dma((9,))] * 8
    scratch += [dma((3, 6))] * 2 + [dma((3,))] * 2 + [dma((3, 8))] * 2 + [dma((8,))] * 2
    scratch += [dma((6,))] * 2 + [dma((3,))] * 2 + [dma((4,))] * 2
    hbm = pl.BlockSpec(memory_space=pl.ANY)
    vmem = pl.BlockSpec(memory_space=pltpu.VMEM)
    return pl.pallas_call(
        kernel,
        out_shape=jax.ShapeDtypeStruct((6144, 384), bf16),
        in_specs=[hbm, hbm, hbm, hbm, vmem, vmem],
        out_specs=hbm,
        scratch_shapes=scratch,
        compiler_params=pltpu.CompilerParams(
            collective_id=0, has_side_effects=True, vmem_limit_bytes=63 * 2**20
        ),
        name="precondition",
    )(
        activations.T, out_grads, basis_in.reshape(8, 48, 6144), basis_out, ein, eig_out.reshape(8, 768)
    )


def solution(mesh):
    in_specs = (P("dp", "owner"), P("dp", None), P("owner", None), P(None, "owner"), P(), P())
    out_specs = P(None, "owner")
    return jax.shard_map(shards, mesh=mesh, in_specs=in_specs, out_specs=out_specs, check_vma=False)
```

time: 526 us -> 310 us (0.59)
  waiting for transfers between devices: 425 us -> 0 us
  Pallas kernels: 0 us -> 298 us
  matrix products: 46.1 us -> 0 us
  blocking collectives: 18.1 us -> 0 us
  between operations: 13.5 us -> 0.03 us
  local copies, waits for them, and re-layouts: 22.6 us -> 10.1 us
    pallas_call x0 -> x1, Pallas kernels: none -> 298 us  [shards(): pl.pallas_call(kernel, out_shape=jax.ShapeDtypeStruct((6144, 384), bf16),...]
    all_gather x3 -> x0, waiting for transfers between devices: 139 us -> none  [the longest x1 58.8 us: shards(): lax.all_gather(grad_cols, 'owner', axis=1, tiled=True)]
    psum x1 -> x0, waiting for transfers between devices: 120 us -> none  [shards(): result = lax.psum(summand.astype(jnp.bfloat16), 'dp')]
    reduce_scatter x1 -> x0, waiting for transfers between devices: 90.3 us -> none  [shards(): lax.psum_scatter(lax.dot_general(out_grads, activations, (((0,), (0,)), (...]
    unnamed x7 -> x0, waiting for transfers between devices: 75.7 us -> none
    dot_general x5 -> x0, matrix products: 46.1 us -> none  [the longest x1 9.88 us: shards(): lax.dot_general(basis_part, scaled, (((1,), (1,)), ((), ())), preferred_e...]
    all_to_all x1 -> x0, blocking collectives: 18.1 us -> none  [shards(): lax.all_to_all(rotated, 'dp', split_axis=0, concat_axis=1, tiled=True)]
    unnamed x8 -> x2, local copies, waits for them, and re-layouts: 18.9 us -> 7.11 us
  transfers between devices with their start and end apart: 6 -> 0, of which waited for: 6 -> 0; matrix products, arithmetic and copies ran while one was open for 7% -> 0% of each run, Pallas kernels for 0% -> 0%
where the time goes in v1:
time: 310 us; the launch traced here: 308 us
  Pallas kernels  298 us (96%)
  local copies, waits for them, and re-layouts  10.1 us (3%)
    pallas_call x1, Pallas kernels, shards(): pl.pallas_call(kernel, out_shape=jax.ShapeDtypeStruct((6144, 384), bf16),...  298 us
    unnamed x2, local copies, waits for them, and re-layouts  7.11 us

profile of v1, /device:TPU:1, one launch (start us, length us, event | category | flops | bytes accessed | tf_op | source)
XLA Modules:
  0.0 308.0 jit_solution(15055134372160579413)
XLA Ops:
  0.0 1.3 reshape.15.eout_ref
  1.3 0.8 reshape.13
  2.2 0.8 copy.9.ein_ref
  3.0 2.1 copy.8
  5.1 297.9 %precondition.1 = bf16[6144,384]{1,0:T(8,128)(2,1)} custom-call(bf16[384,768]{1,0:T(8,128)(2,1)} %bitcast.4, bf16[768,6144]{1,0:T(8,128)(2,1)} %g_ref.1, bf16[8,48,6144]{2,1,0:T(8,128)(2,1)} %bitcast.3, bf16[6144,384]{1,0:T(8,128)(2,1)} %bo_ref.1, f32[8,48,1]{2,1,0:T(8,128)} %copy.9.ein_ref, f32[8,768]{1,0:T(8,128)} %reshape.15.eout_ref), custom_call_target="tpu_custom_call" | custom-call | tf_op jit(solution)/shard_map/precondition/pallas_call | solution.py:488
  303.0 5.0 %copy.11 = bf16[6144,384]{1,0:T(8,128)(2,1)} copy(bf16[6144,384]{1,0:T(8,128)(2,1)} %precondition.1) | data formatting | bytes 9437184
  (1 shorter events, 0.0 us)

commit v2 on v0

v2 whole, which is shorter than its diff:
```python
import jax
import jax.numpy as jnp
from jax import lax
from jax.experimental import pallas as pl
from jax.experimental.pallas import tpu as pltpu
from jax.sharding import PartitionSpec as P

damping = 0.1
bf16 = jnp.bfloat16
f32 = jnp.float32
MESH = pl.DeviceIdType.MESH
parts = 3


def device(yh, z, yl, x, c):
    return (yh * 4 + z, yl * 8 + x * 2 + c)


def remote(src, dst, s, r, dest):
    return pltpu.make_async_remote_copy(src, dst, s, r, device_id=dest, device_id_type=MESH)


class Gather:
    def __init__(self, part, ssem, rsem, p, q, to):
        self.part, self.ssem, self.rsem, self.p, self.q, self.to = part, ssem, rsem, p, q, to

    def copy(self, j, k):
        p, q = self.p, self.q
        o, r, l = 1 - p, (q + 1) % 4, (q + 3) % 4
        pp, qq, half, dest = (
            (p, q, None, (o, q)),
            (p, q, None, (p, r)),
            (p, q, None, (p, l)),
            (o, q, None, (p, r)),
            (o, q, None, (p, l)),
            (p, l, 0, (p, r)),
            (p, r, 1, (p, l)),
            (o, l, 0, (p, r)),
            (o, r, 1, (p, l)),
        )[k]
        ref = self.part(j, pp, qq, half)
        return remote(ref, ref, self.ssem.at[j, k], self.rsem.at[j, k], self.to(*dest))

    def start(self, j, *ks):
        for k in ks:
            self.copy(j, k).start()

    def got(self, j, *ks):
        p, q = self.p, self.q
        o, r, l, a = 1 - p, (q + 1) % 4, (q + 3) % 4, (q + 2) % 4
        for k in ks:
            pp, qq, half = (
                (o, q, None), (p, l, None), (p, r, None), (o, l, None), (o, r, None),
                (p, a, 0), (p, a, 1), (o, a, 0), (o, a, 1),
            )[k]
            ref = self.part(j, pp, qq, half)
            remote(ref, ref, self.ssem.at[j, k], self.rsem.at[j, k], self.to(o, q)).wait_recv()

    def first(self, j):
        self.start(j, 0, 1, 2)

    def second(self, j):
        self.got(j, 0)
        self.start(j, 3, 4)
        self.got(j, 1)
        self.start(j, 5)
        self.got(j, 2)
        self.start(j, 6)

    def third(self, j):
        self.got(j, 3)
        self.start(j, 7)
        self.got(j, 4)
        self.start(j, 8)

    def last(self, j):
        self.got(j, 5, 6, 7, 8)

    def sent(self, j):
        for k in range(9):
            self.copy(j, k).wait_send()


class Reduce:
    def __init__(self, src, bufs, sems, p, q, to):
        self.src, self.p, self.q, self.to = src, p, q, to
        self.mid, self.end, self.out, self.got = bufs
        self.ssem, self.rsem, self.psem, self.qsem = sems

    def copy(self, j, k):
        q = self.q
        r, l, a = (q + 1) % 4, (q + 3) % 4, (q + 2) % 4
        right, left = self.to(self.p, r), self.to(self.p, l)
        src, dst, dest = (
            (self.src.at[j, a, 0], self.mid.at[j, 0], right),
            (self.src.at[j, a, 1], self.mid.at[j, 1], left),
            (self.src.at[j, r, 1], self.end.at[j, 0, 1], right),
            (self.src.at[j, l, 0], self.end.at[j, 1, 0], left),
            (self.src.at[j, r, 0], self.end.at[j, 0, 0], right),
            (self.src.at[j, l, 1], self.end.at[j, 1, 1], left),
        )[k]
        return remote(src, dst, self.ssem.at[j, k], self.rsem.at[j, k], dest)

    def pair(self, j):
        return remote(
            self.out.at[j], self.got.at[j], self.psem.at[j], self.qsem.at[j], self.to(1 - self.p, self.q)
        )

    def far(self, j):
        self.copy(j, 0).start()
        self.copy(j, 1).start()

    def near(self, j):
        self.copy(j, 2).start()
        self.copy(j, 3).start()

    def merge(self, j):
        for h in range(2):
            t = (self.q + 1 + 2 * h) % 4
            self.copy(j, h).wait_recv()
            self.src[j, t, h] = (self.src[j, t, h].astype(f32) + self.mid[j, h].astype(f32)).astype(bf16)
            self.copy(j, 4 + h).start()

    def total(self, j, h):
        return (
            self.src[j, self.q, h].astype(f32) + self.end[j, 0, h].astype(f32) + self.end[j, 1, h].astype(f32)
        )

    def swap(self, j):
        for k in range(2, 6):
            self.copy(j, k).wait_recv()
        self.out[j] = self.total(j, 1 - self.p).astype(bf16)
        self.pair(j).start()

    def result(self, j):
        self.pair(j).wait_recv()
        return self.total(j, self.p) + self.got[j].astype(f32)

    def sent(self, j):
        for k in range(6):
            self.copy(j, k).wait_send()
        self.pair(j).wait_send()


def kernel(
    at_ref, g_ref, bi_ref, bo_ref, ein_ref, eout_ref, o_ref,
    ag, ym, zp, zfull, big, pp, sc, bo, wg, acc, frecv, outg,
    z1, z2, z3, z4, p1, p2, p3, p4, w1, w2, w3, w4,
    lsem, gsem, bsem, tsem, osem,
    a_s, a_r, b_s, b_r, w_s, w_r, o_s, o_r,
    zs, zr, zps, zpr, ps, pr, pps, ppr, xs, xr, xps, xpr, sib_s, sib_r,
):
    rep = lax.axis_index("dp")
    own = lax.axis_index("owner")
    yh, z = rep // 4, rep % 4
    yl, x, c = own // 8, (own // 2) % 4, own % 2
    m = yl * 4 + x
    oc = 1 - c

    sibling = device(yh, z, yl, x, oc)
    over_owner = lambda p, q: device(yh, z, p, q, c)
    over_dp = lambda p, q: device(p, q, yl, x, c)

    barrier = pltpu.get_barrier_semaphore()
    partners = [sibling, over_dp(1 - yh, z), over_owner(1 - yl, x)]
    partners += [over_owner(yl, (x + d) % 4) for d in (1, 3)]
    partners += [over_dp(yh, (z + d) % 4) for d in (1, 3)]
    for dest in partners:
        pl.semaphore_signal(barrier, inc=1, device_id=dest, device_id_type=MESH)

    def wide(k):
        return pl.ds(pl.multiple_of(k * 768, 768), 768)

    def bo_chunk(k):
        return pltpu.make_async_copy(bo_ref.at[wide(k)], bo.at[c, wide(k)], bsem.at[k])

    def g_chunk(k):
        return pltpu.make_async_copy(
            g_ref.at[:, :, :, wide(k)], zp.at[k % 3, pl.ds(0, 3)], gsem.at[k % 3]
        )

    def bi_chunk(j):
        return pltpu.make_async_copy(
            bi_ref.at[j, :, :, wide(rep)], big.at[j, :, pl.ds(pl.multiple_of(m * 16, 16), 16)], tsem.at[j]
        )

    load_a = pltpu.make_async_copy(at_ref, ag.at[:, x, yl], lsem.at[0])
    load_a.start()
    for k in range(3):
        bo_chunk(k).start()
        g_chunk(k).start()
    for k in range(3, 8):
        bo_chunk(k).start()
    for j in range(parts):
        bi_chunk(j).start()

    def rows_half(h, n):
        return pl.ds(0, n) if h is None else pl.ds(h * (n // 2), n // 2)

    ga = Gather(lambda j, p, q, h: ag.at[j, q, p, rows_half(h, 128)], a_s, a_r, yl, x, over_owner)
    gb = Gather(
        lambda j, p, q, h: big.at[j, rows_half(h, 8), pl.ds(pl.multiple_of((p * 4 + q) * 16, 16), 16)],
        b_s, b_r, yl, x, over_owner,
    )
    gw = Gather(lambda j, p, q, h: wg.at[j, q * 2 + p, rows_half(h, 128)], w_s, w_r, yh, z, over_dp)
    go = Gather(lambda j, p, q, h: outg.at[j, q * 2 + p, rows_half(h, 256)], o_s, o_r, yh, z, over_dp)
    wp = zp
    rz = Reduce(zp, (z1, z2, z3, z4), (zs, zr, zps, zpr), yh, z, over_dp)
    rp = Reduce(pp, (p1, p2, p3, p4), (ps, pr, pps, ppr), yh, z, over_dp)
    rw = Reduce(wp, (w1, w2, w3, w4), (xs, xr, xps, xpr), yl, x, over_owner)

    load_a.wait()
    pl.semaphore_wait(barrier, len(partners))
    ga.first(0)
    send_bo = remote(bo_ref, bo.at[c], sib_s.at[0], sib_r.at[0], sibling)

    half = pl.ds(0, 384)
    acc[:, half] = jnp.zeros((768, 384), f32)

    def y_steps(low, high):
        @pl.loop(low, high)
        def _(k):
            bo_chunk(k).wait()
            g_chunk(k).wait()
            part = zp[k % 3, pl.ds(0, 3)].reshape(768, 768)
            acc[:, half] += jnp.dot(part, bo[c, wide(k), :], preferred_element_type=f32)

            @pl.when(k < 5)
            def _():
                g_chunk(k + 3).start()

    mine = pl.ds(pl.multiple_of(c * 384, 128), 384)
    other = pl.ds(pl.multiple_of(oc * 384, 128), 384)
    y_steps(0, 4)
    ga.second(0)
    ga.first(1)
    y_steps(4, 8)
    ym[:, mine] = acc[:, half].astype(bf16)
    send_y = remote(ym.at[:, mine], ym.at[:, mine], sib_s.at[1], sib_r.at[1], sibling)
    send_y.start()
    send_bo.start()
    ga.third(0)
    ga.second(1)
    ga.first(2)
    remote(ym.at[:, other], ym.at[:, other], sib_s.at[1], sib_r.at[1], sibling).wait_recv()

    def unit_dot(lhs, rhs):
        return jnp.dot(lhs.reshape(256, 768), rhs[...], preferred_element_type=f32).astype(bf16).reshape(2, 128, 768)

    def z_part(j):
        for d in (2, 1, 3, 0):
            t = (z + d) % 4
            zp[j, t] = unit_dot(ag[j, t], ym)
            if d == 2:
                rz.far(j)
        rz.near(j)

    def z_done(j):
        rows = pl.ds(pl.multiple_of(c * 384 + j * 128, 128), 128)
        zfull[rows, :] = rz.result(j).astype(bf16)

    ga.last(0)
    z_part(0)
    ga.third(1)
    ga.second(2)
    for j in range(parts):
        bi_chunk(j).wait()
    gb.first(0)
    ga.last(1)
    z_part(1)
    rz.merge(0)
    ga.third(2)
    gb.second(0)
    gb.first(1)
    ga.last(2)
    z_part(2)
    rz.merge(1)
    rz.swap(0)
    gb.third(0)
    gb.second(1)
    gb.first(2)
    rz.merge(2)
    z_done(0)
    rz.swap(1)
    z_done(1)
    gb.third(1)
    gb.second(2)
    rz.swap(2)
    z_done(2)

    def z_rows(core):
        return zfull.at[pl.ds(pl.multiple_of(core * 384, 128), 384)]

    send_z = remote(z_rows(c), z_rows(c), sib_s.at[2], sib_r.at[2], sibling)
    send_z.start()
    gb.third(2)
    for j in range(parts):
        ga.sent(j)
        rz.sent(j)
    remote(z_rows(oc), z_rows(oc), sib_s.at[2], sib_r.at[2], sibling).wait_recv()

    def p_part(j):
        for d in (2, 1, 3, 0):
            t = (z + d) % 4
            pp[j, t] = unit_dot(big[j, pl.ds(2 * t, 2)], zfull)
            if d == 2:
                rp.far(j)
        rp.near(j)

    def p_done(j):
        scale = ein_ref[j] * eout_ref[pl.ds(m, 1), :] + damping
        sc[j] = (rp.result(j) / scale).astype(bf16)

    nt = (((1,), (1,)), ((), ()))

    def w_part(j):
        for d in (2, 1, 3, 0):
            t = (x + d) % 4
            for h in range(2):
                rows = wide(h * 4 + t)
                part = lax.dot_general(sc[j, :, :384], bo[0, rows, :], nt, preferred_element_type=f32)
                part += lax.dot_general(sc[j, :, 384:], bo[1, rows, :], nt, preferred_element_type=f32)
                wp[j, t, h] = part.astype(bf16)
            if d == 2:
                rw.far(j)
        rw.near(j)

    def w_done(j):
        wg[j, z * 2 + yh] = rw.result(j).astype(bf16)
        gw.first(j)

    def out_part(j):
        @pl.loop(0, 4)
        def _(t):
            two = pl.ds(2 * t, 2)
            acc[...] += lax.dot_general(
                big[j, two].reshape(256, 768), wg[j, two].reshape(256, 768), (((0,), (0,)), ((), ())),
                preferred_element_type=f32,
            )

    gb.last(0)
    p_part(0)
    gb.last(1)
    rp.merge(0)
    p_part(1)
    rp.swap(0)
    rp.merge(1)
    gb.last(2)
    p_part(2)
    remote(bo_ref, bo.at[oc], sib_s.at[0], sib_r.at[0], sibling).wait_recv()
    p_done(0)
    w_part(0)
    rp.swap(1)
    rp.merge(2)
    rw.merge(0)
    p_done(1)
    w_part(1)
    rw.swap(0)
    rp.swap(2)
    rw.merge(1)
    w_done(0)
    p_done(2)
    w_part(2)
    acc[...] = jnp.zeros_like(acc)
    gw.second(0)
    rw.swap(1)
    rw.merge(2)
    gw.third(0)
    w_done(1)
    gw.last(0)
    out_part(0)
    gw.second(1)
    rw.swap(2)
    w_done(2)
    gw.third(1)
    gw.second(2)
    gw.last(1)
    out_part(1)
    gw.third(2)
    for j in range(parts):
        gb.sent(j)
        rp.sent(j)
        rw.sent(j)
    gw.last(2)
    out_part(2)

    send_f = remote(acc.at[:, other], frecv, sib_s.at[3], sib_r.at[3], sibling)
    send_f.start()
    remote(frecv, frecv, sib_s.at[3], sib_r.at[3], sibling).wait_recv()

    def o_rows(i):
        return pl.ds(i * 256, 256)

    def store(j, p, q):
        dst = o_ref.at[pl.ds(pl.multiple_of((p * 4 + q) * 768 + j * 256, 256), 256)]
        return pltpu.make_async_copy(outg.at[j, q * 2 + p], dst, osem.at[j, p, q])

    def stores(j, which):
        for dp, dq in which:
            store(j, (yh + dp) % 2, (z + dq) % 4).start()

    near = ((1, 0), (0, 3), (0, 1))
    nearer = ((1, 3), (1, 1))
    far = ((0, 2), (1, 2))
    for j in range(parts):
        outg[j, z * 2 + yh] = (acc[o_rows(j), mine] + frecv[o_rows(j), :]).astype(bf16)
        go.first(j)
        stores(j, ((0, 0),))
        if j >= 1:
            go.second(j - 1)
            stores(j - 1, near)
    go.third(0)
    stores(0, nearer)
    go.second(2)
    stores(2, near)
    go.last(0)
    stores(0, far)
    for j in (1, 2):
        go.third(j)
        stores(j, nearer)
        go.last(j)
        stores(j, far)
    for j in range(parts):
        gw.sent(j)
        go.sent(j)
    for cp in (send_bo, send_y, send_z, send_f):
        cp.wait_send()
    for j in range(parts):
        for p in range(2):
            for q in range(4):
                store(j, p, q).wait()


def shards(activations, out_grads, basis_in, basis_out, eig_in, eig_out):
    rep = lax.axis_index("dp")
    core = lax.axis_index("owner") % 2
    sub = (rep % 4) * 2 + rep // 4
    ein = lax.dynamic_slice(eig_in.reshape(8, 2, 3, 8, 16), (0, core, 0, sub, 0), (8, 1, 3, 1, 16))
    ein = ein.reshape(8, 3, 16).transpose(1, 0, 2).reshape(3, 128, 1)
    dma = pltpu.SemaphoreType.DMA
    v = pltpu.VMEM
    scratch = [
        v((3, 4, 2, 128, 768), bf16), v((768, 768), bf16), v((3, 4, 2, 128, 768), bf16), v((768, 768), bf16),
        v((3, 8, 128, 768), bf16), v((3, 4, 2, 128, 768), bf16), v((3, 128, 768), bf16),
        v((2, 6144, 384), bf16), v((3, 8, 128, 768), bf16), v((768, 768), f32), v((768, 384), f32),
        v((3, 8, 256, 384), bf16),
    ]
    scratch += [
        v((3, 2, 128, 768), bf16), v((3, 2, 2, 128, 768), bf16), v((3, 128, 768), bf16), v((3, 128, 768), bf16)
    ] * 3
    scratch += [dma((1,)), dma((3,)), dma((8,)), dma((3,)), dma((3, 2, 4))]
    scratch += [dma((3, 9))] * 8
    scratch += [dma((3, 6)), dma((3, 6)), dma((3,)), dma((3,))] * 3
    scratch += [dma((4,))] * 2
    hbm = pl.BlockSpec(memory_space=pl.ANY)
    vmem = pl.BlockSpec(memory_space=pltpu.VMEM)
    return pl.pallas_call(
        kernel,
        out_shape=jax.ShapeDtypeStruct((6144, 384), bf16),
        in_specs=[hbm, hbm, hbm, hbm, vmem, vmem],
        out_specs=hbm,
        scratch_shapes=scratch,
        compiler_params=pltpu.CompilerParams(
            collective_id=0, has_side_effects=True, vmem_limit_bytes=63 * 2**20
        ),
        name="precondition",
    )(
        activations.T.reshape(3, 128, 768), out_grads.reshape(3, 2, 128, 6144),
        basis_in.reshape(3, 8, 16, 6144), basis_out, ein, eig_out.reshape(8, 768),
    )


def solution(mesh):
    in_specs = (P("dp", "owner"), P("dp", None), P("owner", None), P(None, "owner"), P(), P())
    out_specs = P(None, "owner")
    return jax.shard_map(shards, mesh=mesh, in_specs=in_specs, out_specs=out_specs, check_vma=False)
```

time: 526 us -> 237 us (0.45)
  waiting for transfers between devices: 425 us -> 0 us
  Pallas kernels: 0 us -> 226 us
  matrix products: 46.1 us -> 0 us
  blocking collectives: 18.1 us -> 0 us
  between operations: 13.5 us -> 0.03 us
  local copies, waits for them, and re-layouts: 22.6 us -> 10.1 us
    pallas_call x0 -> x1, Pallas kernels: none -> 226 us  [shards(): pl.pallas_call(kernel, out_shape=jax.ShapeDtypeStruct((6144, 384), bf16),...]
    all_gather x3 -> x0, waiting for transfers between devices: 139 us -> none  [the longest x1 58.8 us: shards(): lax.all_gather(grad_cols, 'owner', axis=1, tiled=True)]
    psum x1 -> x0, waiting for transfers between devices: 120 us -> none  [shards(): result = lax.psum(summand.astype(jnp.bfloat16), 'dp')]
    reduce_scatter x1 -> x0, waiting for transfers between devices: 90.3 us -> none  [shards(): lax.psum_scatter(lax.dot_general(out_grads, activations, (((0,), (0,)), (...]
    unnamed x7 -> x0, waiting for transfers between devices: 75.7 us -> none
    dot_general x5 -> x0, matrix products: 46.1 us -> none  [the longest x1 9.88 us: shards(): lax.dot_general(basis_part, scaled, (((1,), (1,)), ((), ())), preferred_e...]
    all_to_all x1 -> x0, blocking collectives: 18.1 us -> none  [shards(): lax.all_to_all(rotated, 'dp', split_axis=0, concat_axis=1, tiled=True)]
    unnamed x8 -> x1, local copies, waits for them, and re-layouts: 18.9 us -> 4.99 us
  transfers between devices with their start and end apart: 6 -> 0, of which waited for: 6 -> 0; matrix products, arithmetic and copies ran while one was open for 7% -> 0% of each run, Pallas kernels for 0% -> 0%
where the time goes in v2:
time: 237 us; the launch traced here: 236 us
  Pallas kernels  226 us (95%)
  local copies, waits for them, and re-layouts  10.1 us (4%)
    pallas_call x1, Pallas kernels, shards(): pl.pallas_call(kernel, out_shape=jax.ShapeDtypeStruct((6144, 384), bf16),...  226 us
    unnamed x1, local copies, waits for them, and re-layouts  4.99 us

profile of v2, /device:TPU:1, one launch (start us, length us, event | category | flops | bytes accessed | tf_op | source)
XLA Modules:
  0.0 236.0 jit_solution(18030041027929324646)
XLA Ops:
  0.0 1.3 reshape.27.eout_ref
  1.3 0.8 reshape.24
  2.2 0.8 reshape.28.ein_ref
  3.0 2.1 copy.10
  5.2 225.9 %precondition.1 = bf16[6144,384]{1,0:T(8,128)(2,1)} custom-call(bf16[3,128,768]{2,1,0:T(8,128)(2,1)} %bitcast.11, bf16[3,2,128,6144]{3,2,1,0:T(8,128)(2,1)} %bitcast.9, bf16[3,8,16,6144]{3,2,1,0:T(8,128)(2,1)} %bitcast.10, bf16[6144,384]{1,0:T(8,128)(2,1)} %bo_ref.1, f32[3,128,1]{2,1,0:T(8,128)} %reshape.28.ein_ref, f32[8,768]{1,0:T(8,128)} %reshape.27.eout_ref), custom_call_target="tpu_custom_call" | custom-call | tf_op jit(solution)/shard_map/precondition/pallas_call | solution.py:457
  231.0 5.0 %copy.16 = bf16[6144,384]{1,0:T(8,128)(2,1)} copy(bf16[6144,384]{1,0:T(8,128)(2,1)} %precondition.1) | data formatting | bytes 9437184
  (2 shorter events, 0.0 us)

commit v3 on v0

v3 whole, which is shorter than its diff:
```python
import jax
import jax.numpy as jnp
from jax import lax
from jax.experimental import pallas as pl
from jax.experimental.pallas import tpu as pltpu
from jax.sharding import PartitionSpec as P

damping = 0.1
bf16 = jnp.bfloat16
f32 = jnp.float32
MESH = pl.DeviceIdType.MESH
a_parts, p_parts, b_parts, o_parts = 6, 6, 3, 3
a_rows, p_rows, b_rows, o_rows = 384 // a_parts, 384 // p_parts, 384 // b_parts, 768 // o_parts
a_ways, b_ways, g_ways, o_ways = 'yyyyyy', 'yyy', 'yyyyyy', 'yxy'
order = (
    "A.first.0", "A.first.1", "Y.0", "Y.1", "A.f0.0", "A.f1.0", "A.first.2", "A.f2.0", "Y.2", "A.f0.1",
    "A.f1.1", "A.first.3", "A.f2.1", "Y.3", "Y.4", "A.f3.0", "A.f4.0", "A.f0.2", "Y.5", "A.f2.2", "A.f0.3",
    "Y.6", "A.f1.2", "A.first.4", "Y.7", "A.f3.1", "A.f4.1", "yout", "A.f2.3", "A.f0.4", "A.f1.3",
    "A.first.5", "Zc.0", "Z.go.0", "A.f3.2", "A.f4.2", "A.f0.5", "A.f3.3", "A.f4.3", "Z.m0.0", "Z.m1.0",
    "A.f1.4", "A.f2.4", "Zc.1", "Z.go.1", "Z.swap.0", "A.f3.4", "A.f4.4", "Z.m0.1", "Z.m1.1", "A.f1.5",
    "A.f2.5", "Zr.0", "Zc.2", "Z.go.2", "A.f3.5", "A.f4.5", "B.first.0", "Z.swap.1", "Zc.3", "Z.m0.2",
    "Z.m1.2", "Z.go.3", "Zc.4", "Zc.5", "B.f0.0", "Z.swap.2", "Zr.1", "Z.m0.3", "Z.m1.3", "Z.go.4", "B.f1.0",
    "B.first.1", "B.f2.0", "Zr.2", "Z.swap.3", "B.f3.0", "B.f4.0", "Z.m0.4", "Z.m1.4", "B.f0.1", "Z.go.5",
    "Zr.3", "B.f2.1", "Z.swap.4", "B.f1.1", "B.first.2", "Z.m0.5", "Z.m1.5", "Zr.4", "Z.swap.5", "B.f3.1",
    "B.f4.1", "B.f0.2", "Zr.5", "Pc.0", "B.f1.2", "B.f2.2", "P.go.0", "Pc.1", "Pc.2", "Pc.3", "P.m0.0",
    "P.m1.0", "P.go.1", "B.f3.2", "B.f4.2", "P.swap.0", "P.m0.1", "P.m1.1", "P.go.2", "Pc.4", "Pc.5", "Pr.0",
    "Wc.0", "W.go.0", "P.swap.1", "P.m0.2", "P.m1.2", "P.go.3", "W.m0.0", "W.m1.0", "Pr.1", "Wc.1", "W.go.1",
    "P.swap.2", "P.m0.3", "P.m1.3", "P.go.4", "W.swap.0", "W.m0.1", "W.m1.1", "Pr.2", "Wc.2", "P.m0.4",
    "P.m1.4", "P.go.5", "W.go.2", "P.swap.3", "Wr.0", "G.first.0", "W.swap.1", "P.swap.4", "W.m0.2", "W.m1.2",
    "Pr.3", "Wc.3", "P.m0.5", "P.m1.5", "G.f0.0", "W.go.3", "W.swap.2", "Wr.1", "G.first.1", "G.f1.0",
    "G.f2.0", "Pr.4", "Wc.4", "W.m0.3", "W.m1.3", "W.go.4", "P.swap.5", "Wr.2", "G.first.2", "G.f3.0",
    "G.f4.0", "G.f0.1", "G.f1.1", "G.f2.1", "W.swap.3", "Pr.5", "Wc.5", "W.m0.4", "W.m1.4", "G.f1.2",
    "G.f2.2", "G.f0.2", "W.go.5", "Oc.0", "Wr.3", "G.first.3", "G.f3.1", "G.f4.1", "W.swap.4", "W.m0.5",
    "W.m1.5", "G.f0.3", "G.f3.2", "G.f4.2", "Wr.4", "G.first.4", "G.f1.3", "G.f2.3", "Oc.1", "W.swap.5",
    "G.f3.3", "G.f4.3", "G.f0.4", "Oc.2", "Wr.5", "G.first.5", "G.f1.4", "G.f2.4", "Oc.3", "G.f0.5", "G.f3.4",
    "G.f4.4", "G.f1.5", "G.f2.5", "G.f3.5", "G.f4.5", "Oc.4", "Oc.5", "fsend", "osum.0", "O.first.0",
    "osum.1", "O.first.1", "osum.2", "O.first.2", "O.f0.0", "O.f1.0", "O.f2.0", "O.f0.1", "O.f1.1", "O.f0.2",
    "O.f1.2", "O.f2.2", "O.f3.0", "O.f4.0", "O.f2.1", "O.f3.2", "O.f4.2",
)


def device(yh, z, yl, x, c):
    return (yh * 4 + z, yl * 8 + x * 2 + c)


def remote(src, dst, s, r, dest):
    return pltpu.make_async_remote_copy(src, dst, s, r, device_id=dest, device_id_type=MESH)


class Gather:
    def __init__(self, part, ways, ssem, rsem, p, q, to):
        self.part, self.ways, self.ssem, self.rsem, self.p, self.q, self.to = part, ways, ssem, rsem, p, q, to

    def plan(self, j):
        p, q = self.p, self.q
        o, r, l, a = 1 - p, (q + 1) % 4, (q + 3) % 4, (q + 2) % 4
        if self.ways[j] == "y":
            return (
                ((p, q, None), (o, q), (o, q, None)),
                ((p, q, None), (p, r), (p, l, None)),
                ((p, q, None), (p, l), (p, r, None)),
                ((o, q, None), (p, r), (o, l, None)),
                ((o, q, None), (p, l), (o, r, None)),
                ((p, l, 0), (p, r), (p, a, 0)),
                ((p, r, 1), (p, l), (p, a, 1)),
                ((o, l, 0), (p, r), (o, a, 0)),
                ((o, r, 1), (p, l), (o, a, 1)),
            )
        return (
            ((p, q, None), (p, r), (p, l, None)),
            ((p, q, None), (p, l), (p, r, None)),
            ((p, l, 0), (p, r), (p, a, 0)),
            ((p, r, 1), (p, l), (p, a, 1)),
            ((p, q, None), (o, q), (o, q, None)),
            ((p, l, None), (o, q), (o, l, None)),
            ((p, r, None), (o, q), (o, r, None)),
            ((p, a, None), (o, q), (o, a, None)),
        )

    def copy(self, j, k):
        block, dest, _ = self.plan(j)[k]
        ref = self.part(j, *block)
        return remote(ref, ref, self.ssem.at[j, k], self.rsem.at[j, k], self.to(*dest))

    def start(self, j, *ks):
        for k in ks:
            self.copy(j, k).start()

    def got(self, j, *ks):
        for k in ks:
            _, dest, block = self.plan(j)[k]
            ref = self.part(j, *block)
            remote(ref, ref, self.ssem.at[j, k], self.rsem.at[j, k], self.to(*dest)).wait_recv()

    def step(self, what, j):
        if self.ways[j] == "y":
            waits, starts = {
                "first": ((), (0, 1, 2)),
                "f0": ((0,), (3, 4)),
                "f1": ((1,), (5,)),
                "f2": ((2,), (6,)),
                "f3": ((3,), (7,)),
                "f4": ((4,), (8,)),
                "last": ((5, 6, 7, 8), ()),
            }[what]
        else:
            waits, starts = {
                "first": ((), (0, 1, 4)),
                "f0": ((0,), (2, 5)),
                "f1": ((1,), (3, 6)),
                "f2": ((2, 3), (7,)),
                "last": ((4, 5, 6, 7), ()),
            }[what]
        self.got(j, *waits)
        self.start(j, *starts)

    def sent(self):
        for j in range(len(self.ways)):
            for k in range(len(self.plan(j))):
                self.copy(j, k).wait_send()


class Reduce:
    def __init__(self, n, src, bufs, sems, p, q, to):
        self.n, self.src, self.p, self.q, self.to = n, src, p, q, to
        self.mid, self.end, self.out, self.got = bufs
        self.ssem, self.rsem, self.psem, self.qsem = sems

    def copy(self, j, k):
        q = self.q
        r, l, a = (q + 1) % 4, (q + 3) % 4, (q + 2) % 4
        right, left = self.to(self.p, r), self.to(self.p, l)
        src, dst, dest = (
            (self.src.at[j, a, 0], self.mid.at[j, 0], right),
            (self.src.at[j, a, 1], self.mid.at[j, 1], left),
            (self.src.at[j, r, 1], self.end.at[j, 0, 1], right),
            (self.src.at[j, l, 0], self.end.at[j, 1, 0], left),
            (self.src.at[j, r, 0], self.end.at[j, 0, 0], right),
            (self.src.at[j, l, 1], self.end.at[j, 1, 1], left),
        )[k]
        return remote(src, dst, self.ssem.at[j, k], self.rsem.at[j, k], dest)

    def pair(self, j):
        return remote(
            self.out.at[j], self.got.at[j], self.psem.at[j], self.qsem.at[j], self.to(1 - self.p, self.q)
        )

    def total(self, j, h):
        return (
            self.src[j, self.q, h].astype(f32) + self.end[j, 0, h].astype(f32) + self.end[j, 1, h].astype(f32)
        )

    def step(self, what, j):
        if what == "go":
            for k in range(4):
                self.copy(j, k).start()
        elif what == "swap":
            for k in range(2, 6):
                self.copy(j, k).wait_recv()
            self.out[j] = self.total(j, 1 - self.p).astype(bf16)
            self.pair(j).start()
        else:
            h = 0 if what == "m0" else 1
            t = (self.q + 1 + 2 * h) % 4
            self.copy(j, h).wait_recv()
            self.src[j, t, h] = (self.src[j, t, h].astype(f32) + self.mid[j, h].astype(f32)).astype(bf16)
            self.copy(j, 4 + h).start()

    def result(self, j):
        self.pair(j).wait_recv()
        return self.total(j, self.p) + self.got[j].astype(f32)

    def sent(self):
        for j in range(self.n):
            for k in range(6):
                self.copy(j, k).wait_send()
            self.pair(j).wait_send()


def kernel(
    at_ref, g_ref, bi_ref, bo_ref, ein_ref, eout_ref, o_ref,
    ag, ym, zp, zfull, big, pp, sc, bo, wp, wg, acc, frecv, outg,
    z1, z2, z3, z4, p1, p2, p3, p4, w1, w2, w3, w4,
    lsem, gsem, bsem, tsem, osem,
    a_s, a_r, b_s, b_r, w_s, w_r, o_s, o_r,
    zs, zr, zps, zpr, ps, pr, pps, ppr, xs, xr, xps, xpr, sib_s, sib_r, zsib_s, zsib_r,
):
    rep = lax.axis_index("dp")
    own = lax.axis_index("owner")
    yh, z = rep // 4, rep % 4
    yl, x, c = own // 8, (own // 2) % 4, own % 2
    m = yl * 4 + x
    oc = 1 - c

    sibling = device(yh, z, yl, x, oc)
    over_owner = lambda p, q: device(yh, z, p, q, c)
    over_dp = lambda p, q: device(p, q, yl, x, c)

    barrier = pltpu.get_barrier_semaphore()
    partners = [sibling, over_dp(1 - yh, z), over_owner(1 - yl, x)]
    partners += [over_owner(yl, (x + d) % 4) for d in (1, 3)]
    partners += [over_dp(yh, (z + d) % 4) for d in (1, 3)]
    for dest in partners:
        pl.semaphore_signal(barrier, inc=1, device_id=dest, device_id_type=MESH)

    def at(start, size, step):
        return pl.ds(pl.multiple_of(start, step), size)

    def wide(k):
        return at(k * 768, 768, 768)

    def halves(h, n):
        return pl.ds(0, n) if h is None else pl.ds(h * (n // 2), n // 2)

    def bo_chunk(k):
        return pltpu.make_async_copy(bo_ref.at[wide(k)], bo.at[c, wide(k)], bsem.at[k])

    def g_chunk(k):
        b = k % 4
        return pltpu.make_async_copy(g_ref.at[:, :, :, wide(k)], wg.at[:, pl.ds(2 * b, 2)], gsem.at[b])

    def bi_chunk(j):
        return pltpu.make_async_copy(
            bi_ref.at[j, :, :, wide(rep)], big.at[j, :, at(m * 16, 16, 16)], tsem.at[j]
        )

    load_a = pltpu.make_async_copy(at_ref, ag.at[:, x, yl], lsem.at[0])
    load_a.start()
    for k in range(4):
        bo_chunk(k).start()
        g_chunk(k).start()
    for k in range(4, 8):
        bo_chunk(k).start()
    for j in range(b_parts):
        bi_chunk(j).start()

    ga = Gather(lambda j, p, q, h: ag.at[j, q, p, halves(h, a_rows)], a_ways, a_s, a_r, yl, x, over_owner)
    gb = Gather(
        lambda j, p, q, h: big.at[j, halves(h, 8), at((p * 4 + q) * 16, 16, 16)],
        b_ways, b_s, b_r, yl, x, over_owner,
    )
    gw = Gather(lambda j, p, q, h: wg.at[j, q * 2 + p, halves(h, p_rows)], g_ways, w_s, w_r, yh, z, over_dp)
    go = Gather(lambda j, p, q, h: outg.at[j, q * 2 + p, halves(h, o_rows)], o_ways, o_s, o_r, yh, z, over_dp)
    rz = Reduce(a_parts, zp, (z1, z2, z3, z4), (zs, zr, zps, zpr), yh, z, over_dp)
    rp = Reduce(p_parts, pp, (p1, p2, p3, p4), (ps, pr, pps, ppr), yh, z, over_dp)
    rw = Reduce(p_parts, wp, (w1, w2, w3, w4), (xs, xr, xps, xpr), yl, x, over_owner)

    half = pl.ds(0, 384)
    mine, other = at(c * 384, 384, 128), at(oc * 384, 384, 128)
    send_bo = remote(bo_ref, bo.at[c], sib_s.at[0], sib_r.at[0], sibling)
    send_y = remote(ym.at[:, mine], ym.at[:, mine], sib_s.at[1], sib_r.at[1], sibling)
    send_f = remote(acc.at[:, other], frecv, sib_s.at[2], sib_r.at[2], sibling)
    group = p_parts // b_parts
    nt = (((1,), (1,)), ((), ()))
    tn = (((0,), (0,)), ((), ()))

    def y_step(k):
        bo_chunk(k).wait()
        g_chunk(k).wait()
        b = k % 4
        lhs = wg[:, pl.ds(2 * b, 2)].reshape(768, 768)
        part = jnp.dot(lhs, bo[c, wide(k), :], preferred_element_type=f32)
        acc[:, half] = part if k == 0 else acc[:, half] + part
        if k + 4 < 8:
            g_chunk(k + 4).start()

    def y_out():
        ym[:, mine] = acc[:, half].astype(bf16)
        send_y.start()
        send_bo.start()

    def z_part(j):
        if j == 0:
            remote(ym.at[:, other], ym.at[:, other], sib_s.at[1], sib_r.at[1], sibling).wait_recv()
        ga.step("last", j)

        @pl.loop(0, 2)
        def _(t):
            two = pl.ds(2 * t, 2)
            part = jnp.dot(ag[j, two].reshape(4 * a_rows, 768), ym[...], preferred_element_type=f32)
            zp[j, two] = part.astype(bf16).reshape(2, 2, a_rows, 768)

    def z_copy(j, core):
        ref = zfull.at[at(core * 384 + j * a_rows, a_rows, a_rows)]
        return remote(ref, ref, zsib_s.at[j], zsib_r.at[j], sibling)

    def z_done(j):
        zfull[at(c * 384 + j * a_rows, a_rows, a_rows), :] = rz.result(j).astype(bf16)
        z_copy(j, c).start()

    def p_part(j):
        if j == 0:
            for i in range(a_parts):
                z_copy(i, oc).wait_recv()
        if j % group == 0:
            gb.step("last", j // group)
        rows = pl.ds((j % group) * p_rows, p_rows)

        @pl.loop(0, 2)
        def _(t):
            lhs = big[j // group, pl.ds(4 * t, 4), rows, :].reshape(4 * p_rows, 768)
            part = jnp.dot(lhs, zfull[...], preferred_element_type=f32)
            pp[j, pl.ds(2 * t, 2)] = part.astype(bf16).reshape(2, 2, p_rows, 768)

    def p_done(j):
        scale = ein_ref[j] * eout_ref[pl.ds(m, 1), :] + damping
        sc[j] = (rp.result(j) / scale).astype(bf16)

    def w_part(j):
        if j == 0:
            remote(bo_ref, bo.at[oc], sib_s.at[0], sib_r.at[0], sibling).wait_recv()

        @pl.loop(0, 8)
        def _(t):
            rows = wide((t % 2) * 4 + t // 2)
            part = lax.dot_general(sc[j, :, :384], bo[0, rows, :], nt, preferred_element_type=f32)
            part += lax.dot_general(sc[j, :, 384:], bo[1, rows, :], nt, preferred_element_type=f32)
            wp[j, t // 2, t % 2] = part.astype(bf16)

    def w_done(j):
        wg[j, z * 2 + yh] = rw.result(j).astype(bf16)

    def out_part(j):
        gw.step("last", j)
        rows = pl.ds((j % group) * p_rows, p_rows)
        lhs = big[j // group, :, rows, :].reshape(8 * p_rows, 768)
        part = lax.dot_general(lhs, wg[j].reshape(8 * p_rows, 768), tn, preferred_element_type=f32)
        acc[...] = part if j == 0 else acc[...] + part

    def store(j, p, q):
        dst = o_ref.at[at((p * 4 + q) * 768 + j * o_rows, o_rows, o_rows)]
        return pltpu.make_async_copy(outg.at[j, q * 2 + p], dst, osem.at[j, p, q])

    def out_sum(j):
        if j == 0:
            remote(frecv, frecv, sib_s.at[2], sib_r.at[2], sibling).wait_recv()
        rows = pl.ds(j * o_rows, o_rows)
        outg[j, z * 2 + yh] = (acc[rows, mine] + frecv[rows, :]).astype(bf16)

    others = {
        "Zc": z_part, "Zr": z_done, "Pc": p_part, "Pr": p_done, "Wc": w_part, "Wr": w_done, "Oc": out_part,
        "osum": out_sum, "Y": y_step,
    }
    movers = {"A": ga, "B": gb, "G": gw, "O": go, "Z": rz, "P": rp, "W": rw}

    load_a.wait()
    pl.semaphore_wait(barrier, len(partners))
    for step in order:
        name = step.split(".")
        if name[0] in others:
            others[name[0]](int(name[1]))
        elif name[0] in movers:
            if name[0] == "B" and name[1] == "first":
                bi_chunk(int(name[2])).wait()
            movers[name[0]].step(name[1], int(name[2]))
        elif step == "yout":
            y_out()
        else:
            send_f.start()

    for dp, dq in ((0, 0), (1, 0), (0, 1), (0, 3), (1, 1), (1, 3), (0, 2), (1, 2)):
        if (dp, dq) == (1, 0):
            for j in range(o_parts):
                go.step("last", j)
        for j in range(o_parts):
            store(j, (yh + dp) % 2, (z + dq) % 4).start()
    for mover in (ga, gb, gw, go, rz, rp, rw):
        mover.sent()
    for cp in (send_bo, send_y, send_f):
        cp.wait_send()
    for j in range(a_parts):
        z_copy(j, c).wait_send()
    for j in range(o_parts):
        for p in range(2):
            for q in range(4):
                store(j, p, q).wait()


def shards(activations, out_grads, basis_in, basis_out, eig_in, eig_out):
    rep = lax.axis_index("dp")
    core = lax.axis_index("owner") % 2
    sub = (rep % 4) * 2 + rep // 4
    ein = lax.dynamic_slice(eig_in.reshape(8, 2, 3, 8, 16), (0, core, 0, sub, 0), (8, 1, 3, 1, 16))
    ein = ein.reshape(8, 3, 16).transpose(1, 0, 2).reshape(p_parts, p_rows, 1)
    dma = pltpu.SemaphoreType.DMA
    v = pltpu.VMEM
    scratch = [
        v((a_parts, 4, 2, a_rows, 768), bf16), v((768, 768), bf16), v((a_parts, 4, 2, a_rows, 768), bf16),
        v((768, 768), bf16), v((b_parts, 8, b_rows, 768), bf16), v((p_parts, 4, 2, p_rows, 768), bf16),
        v((p_parts, p_rows, 768), bf16), v((2, 6144, 384), bf16), v((p_parts, 4, 2, p_rows, 768), bf16),
        v((p_parts, 8, p_rows, 768), bf16), v((768, 768), f32), v((768, 384), f32),
        v((o_parts, 8, o_rows, 384), bf16),
    ]
    for n, rows in ((a_parts, a_rows), (p_parts, p_rows), (p_parts, p_rows)):
        scratch += [
            v((n, 2, rows, 768), bf16), v((n, 2, 2, rows, 768), bf16), v((n, rows, 768), bf16),
            v((n, rows, 768), bf16),
        ]
    scratch += [dma((1,)), dma((4,)), dma((8,)), dma((b_parts,)), dma((o_parts, 2, 4))]
    for n in (a_parts, b_parts, p_parts, o_parts):
        scratch += [dma((n, 9))] * 2
    for n in (a_parts, p_parts, p_parts):
        scratch += [dma((n, 6))] * 2 + [dma((n,))] * 2
    scratch += [dma((3,))] * 2 + [dma((a_parts,))] * 2
    hbm = pl.BlockSpec(memory_space=pl.ANY)
    vmem = pl.BlockSpec(memory_space=pltpu.VMEM)
    return pl.pallas_call(
        kernel,
        out_shape=jax.ShapeDtypeStruct((6144, 384), bf16),
        in_specs=[hbm, hbm, hbm, hbm, vmem, vmem],
        out_specs=hbm,
        scratch_shapes=scratch,
        compiler_params=pltpu.CompilerParams(
            collective_id=0, has_side_effects=True, vmem_limit_bytes=64 * 2**20
        ),
        name="precondition",
    )(
        activations.T.reshape(a_parts, a_rows, 768), out_grads.reshape(p_parts, 2, p_rows, 6144),
        basis_in.reshape(b_parts, 8, 16, 6144), basis_out, ein, eig_out.reshape(8, 768),
    )


def solution(mesh):
    in_specs = (P("dp", "owner"), P("dp", None), P("owner", None), P(None, "owner"), P(), P())
    out_specs = P(None, "owner")
    return jax.shard_map(shards, mesh=mesh, in_specs=in_specs, out_specs=out_specs, check_vma=False)
```

time: 526 us -> 219 us (0.42)
  waiting for transfers between devices: 425 us -> 0 us
  Pallas kernels: 0 us -> 208 us
  matrix products: 46.1 us -> 0 us
  blocking collectives: 18.1 us -> 0 us
  between operations: 13.5 us -> 0.03 us
  local copies, waits for them, and re-layouts: 22.6 us -> 10.1 us
    pallas_call x0 -> x1, Pallas kernels: none -> 208 us  [shards(): pl.pallas_call(kernel, out_shape=jax.ShapeDtypeStruct((6144, 384), bf16),...]
    all_gather x3 -> x0, waiting for transfers between devices: 139 us -> none  [the longest x1 58.8 us: shards(): lax.all_gather(grad_cols, 'owner', axis=1, tiled=True)]
    psum x1 -> x0, waiting for transfers between devices: 120 us -> none  [shards(): result = lax.psum(summand.astype(jnp.bfloat16), 'dp')]
    reduce_scatter x1 -> x0, waiting for transfers between devices: 90.3 us -> none  [shards(): lax.psum_scatter(lax.dot_general(out_grads, activations, (((0,), (0,)), (...]
    unnamed x7 -> x0, waiting for transfers between devices: 75.7 us -> none
    dot_general x5 -> x0, matrix products: 46.1 us -> none  [the longest x1 9.88 us: shards(): lax.dot_general(basis_part, scaled, (((1,), (1,)), ((), ())), preferred_e...]
    all_to_all x1 -> x0, blocking collectives: 18.1 us -> none  [shards(): lax.all_to_all(rotated, 'dp', split_axis=0, concat_axis=1, tiled=True)]
    unnamed x8 -> x1, local copies, waits for them, and re-layouts: 18.9 us -> 4.99 us
  transfers between devices with their start and end apart: 6 -> 0, of which waited for: 6 -> 0; matrix products, arithmetic and copies ran while one was open for 7% -> 0% of each run, Pallas kernels for 0% -> 0%
where the time goes in v3:
time: 219 us
  Pallas kernels  208 us (95%)
  local copies, waits for them, and re-layouts  10.1 us (5%)
    pallas_call x1, Pallas kernels, shards(): pl.pallas_call(kernel, out_shape=jax.ShapeDtypeStruct((6144, 384), bf16),...  208 us
    unnamed x1, local copies, waits for them, and re-layouts  4.99 us

profile of v3, /device:TPU:1, one launch (start us, length us, event | category | flops | bytes accessed | tf_op | source)
XLA Modules:
  0.0 218.5 jit_solution(45006941938190483)
XLA Ops:
  0.0 1.3 reshape.27.eout_ref
  1.3 0.8 reshape.24
  2.2 0.8 reshape.28.ein_ref
  3.0 2.1 copy.10
  5.2 208.3 %precondition.1 = bf16[6144,384]{1,0:T(8,128)(2,1)} custom-call(bf16[6,64,768]{2,1,0:T(8,128)(2,1)} %bitcast.11, bf16[6,2,64,6144]{3,2,1,0:T(8,128)(2,1)} %bitcast.9, bf16[3,8,16,6144]{3,2,1,0:T(8,128)(2,1)} %bitcast.10, bf16[6144,384]{1,0:T(8,128)(2,1)} %bo_ref.1, f32[6,64,1]{2,1,0:T(8,128)} %reshape.28.ein_ref, f32[8,768]{1,0:T(8,128)} %reshape.27.eout_ref), custom_call_target="tpu_custom_call" | custom-call | tf_op jit(solution)/shard_map/precondition/pallas_call | solution.py:407
  213.5 5.0 %copy.16 = bf16[6144,384]{1,0:T(8,128)(2,1)} copy(bf16[6144,384]{1,0:T(8,128)(2,1)} %precondition.1) | data formatting | bytes 9437184
  (2 shorter events, 0.0 us)

commit v4 on v3

--- a/solution.py
+++ b/solution.py
@@ -11,31 +11,25 @@
 MESH = pl.DeviceIdType.MESH
 a_parts, p_parts, b_parts, o_parts = 6, 6, 3, 3
 a_rows, p_rows, b_rows, o_rows = 384 // a_parts, 384 // p_parts, 384 // b_parts, 768 // o_parts
-a_ways, b_ways, g_ways, o_ways = 'yyyyyy', 'yyy', 'yyyyyy', 'yxy'
+a_ways, b_ways, g_ways, o_ways = 'yxyyxy', 'yyy', 'yyyyyy', 'yxy'
+steps = (
+    "A.first", "Y", "A.f0", "A.f1", "A.f2", "A.f3", "A.f4", "yout", "T", "Zc", "Z.go", "Z.m0", "Z.m1", "Z.swap",
+    "Zr", "B.first", "B.f0", "B.f1", "B.f2", "B.f3", "B.f4", "Pc", "P.go", "P.m0", "P.m1", "P.swap", "Pr", "Wc",
+    "W.go", "W.m0", "W.m1", "W.swap", "Wr", "G.first", "G.f0", "G.f1", "G.f2", "G.f3", "G.f4", "Oc", "fsend",
+    "osum", "O.first", "O.f0", "O.f1", "O.f2", "O.f3", "O.f4",
+)
 order = (
-    "A.first.0", "A.first.1", "Y.0", "Y.1", "A.f0.0", "A.f1.0", "A.first.2", "A.f2.0", "Y.2", "A.f0.1",
-    "A.f1.1", "A.first.3", "A.f2.1", "Y.3", "Y.4", "A.f3.0", "A.f4.0", "A.f0.2", "Y.5", "A.f2.2", "A.f0.3",
-    "Y.6", "A.f1.2", "A.first.4", "Y.7", "A.f3.1", "A.f4.1", "yout", "A.f2.3", "A.f0.4", "A.f1.3",
-    "A.first.5", "Zc.0", "Z.go.0", "A.f3.2", "A.f4.2", "A.f0.5", "A.f3.3", "A.f4.3", "Z.m0.0", "Z.m1.0",
-    "A.f1.4", "A.f2.4", "Zc.1", "Z.go.1", "Z.swap.0", "A.f3.4", "A.f4.4", "Z.m0.1", "Z.m1.1", "A.f1.5",
-    "A.f2.5", "Zr.0", "Zc.2", "Z.go.2", "A.f3.5", "A.f4.5", "B.first.0", "Z.swap.1", "Zc.3", "Z.m0.2",
-    "Z.m1.2", "Z.go.3", "Zc.4", "Zc.5", "B.f0.0", "Z.swap.2", "Zr.1", "Z.m0.3", "Z.m1.3", "Z.go.4", "B.f1.0",
-    "B.first.1", "B.f2.0", "Zr.2", "Z.swap.3", "B.f3.0", "B.f4.0", "Z.m0.4", "Z.m1.4", "B.f0.1", "Z.go.5",
-    "Zr.3", "B.f2.1", "Z.swap.4", "B.f1.1", "B.first.2", "Z.m0.5", "Z.m1.5", "Zr.4", "Z.swap.5", "B.f3.1",
-    "B.f4.1", "B.f0.2", "Zr.5", "Pc.0", "B.f1.2", "B.f2.2", "P.go.0", "Pc.1", "Pc.2", "Pc.3", "P.m0.0",
-    "P.m1.0", "P.go.1", "B.f3.2", "B.f4.2", "P.swap.0", "P.m0.1", "P.m1.1", "P.go.2", "Pc.4", "Pc.5", "Pr.0",
-    "Wc.0", "W.go.0", "P.swap.1", "P.m0.2", "P.m1.2", "P.go.3", "W.m0.0", "W.m1.0", "Pr.1", "Wc.1", "W.go.1",
-    "P.swap.2", "P.m0.3", "P.m1.3", "P.go.4", "W.swap.0", "W.m0.1", "W.m1.1", "Pr.2", "Wc.2", "P.m0.4",
-    "P.m1.4", "P.go.5", "W.go.2", "P.swap.3", "Wr.0", "G.first.0", "W.swap.1", "P.swap.4", "W.m0.2", "W.m1.2",
-    "Pr.3", "Wc.3", "P.m0.5", "P.m1.5", "G.f0.0", "W.go.3", "W.swap.2", "Wr.1", "G.first.1", "G.f1.0",
-    "G.f2.0", "Pr.4", "Wc.4", "W.m0.3", "W.m1.3", "W.go.4", "P.swap.5", "Wr.2", "G.first.2", "G.f3.0",
-    "G.f4.0", "G.f0.1", "G.f1.1", "G.f2.1", "W.swap.3", "Pr.5", "Wc.5", "W.m0.4", "W.m1.4", "G.f1.2",
-    "G.f2.2", "G.f0.2", "W.go.5", "Oc.0", "Wr.3", "G.first.3", "G.f3.1", "G.f4.1", "W.swap.4", "W.m0.5",
-    "W.m1.5", "G.f0.3", "G.f3.2", "G.f4.2", "Wr.4", "G.first.4", "G.f1.3", "G.f2.3", "Oc.1", "W.swap.5",
-    "G.f3.3", "G.f4.3", "G.f0.4", "Oc.2", "Wr.5", "G.first.5", "G.f1.4", "G.f2.4", "Oc.3", "G.f0.5", "G.f3.4",
-    "G.f4.4", "G.f1.5", "G.f2.5", "G.f3.5", "G.f4.5", "Oc.4", "Oc.5", "fsend", "osum.0", "O.first.0",
-    "osum.1", "O.first.1", "osum.2", "O.first.2", "O.f0.0", "O.f1.0", "O.f2.0", "O.f0.1", "O.f1.1", "O.f0.2",
-    "O.f1.2", "O.f2.2", "O.f3.0", "O.f4.0", "O.f2.1", "O.f3.2", "O.f4.2",
+    0, 1, 16, 17, 18, 32, 48, 2, 64, 19, 20, 33, 49, 3, 21, 22, 80, 96, 34, 23, 112, 66, 50, 4, 128, 65, 129,
+    130, 131, 51, 67, 35, 5, 144, 160, 82, 98, 145, 176, 192, 161, 36, 52, 37, 83, 99, 208, 53, 69, 177, 193,
+    146, 68, 162, 224, 85, 101, 240, 209, 147, 148, 178, 194, 163, 149, 256, 210, 272, 241, 288, 225, 179, 195,
+    164, 226, 304, 320, 211, 257, 180, 196, 165, 289, 227, 273, 242, 212, 181, 197, 258, 305, 321, 213, 228,
+    229, 274, 290, 336, 352, 337, 306, 322, 368, 384, 353, 338, 339, 400, 340, 341, 369, 385, 354, 416, 432,
+    448, 401, 370, 386, 355, 464, 480, 417, 433, 371, 387, 356, 449, 402, 496, 403, 465, 481, 418, 434, 372,
+    388, 357, 450, 512, 528, 497, 419, 435, 466, 482, 544, 451, 404, 373, 389, 513, 529, 498, 420, 436, 560,
+    576, 467, 483, 545, 592, 608, 452, 514, 530, 405, 561, 577, 499, 546, 468, 484, 593, 609, 421, 437, 562,
+    578, 453, 515, 531, 500, 624, 594, 610, 625, 469, 485, 547, 563, 579, 516, 532, 626, 501, 595, 611, 548,
+    564, 580, 517, 533, 627, 596, 612, 549, 565, 581, 628, 597, 613, 629, 640, 656, 672, 657, 673, 658, 674,
+    688, 704, 720, 689, 705, 690, 706, 722, 736, 752, 721, 738, 754,
 )
 
 
@@ -121,8 +115,8 @@
 
 
 class Reduce:
-    def __init__(self, n, src, bufs, sems, p, q, to):
-        self.n, self.src, self.p, self.q, self.to = n, src, p, q, to
+    def __init__(self, src, bufs, sems, p, q, to):
+        self.src, self.p, self.q, self.to = src, p, q, to
         self.mid, self.end, self.out, self.got = bufs
         self.ssem, self.rsem, self.psem, self.qsem = sems
 
@@ -163,23 +157,22 @@
             h = 0 if what == "m0" else 1
             t = (self.q + 1 + 2 * h) % 4
             self.copy(j, h).wait_recv()
-            self.src[j, t, h] = (self.src[j, t, h].astype(f32) + self.mid[j, h].astype(f32)).astype(bf16)
+            self.src[j, t, h] = self.src[j, t, h] + self.mid[j, h]
             self.copy(j, 4 + h).start()
 
     def result(self, j):
         self.pair(j).wait_recv()
         return self.total(j, self.p) + self.got[j].astype(f32)
 
-    def sent(self):
-        for j in range(self.n):
-            for k in range(6):
-                self.copy(j, k).wait_send()
-            self.pair(j).wait_send()
+    def sent(self, j):
+        for k in range(6):
+            self.copy(j, k).wait_send()
+        self.pair(j).wait_send()
 
 
 def kernel(
-    at_ref, g_ref, bi_ref, bo_ref, ein_ref, eout_ref, o_ref,
-    ag, ym, zp, zfull, big, pp, sc, bo, wp, wg, acc, frecv, outg,
+    a_ref, g_ref, bi_ref, bo_ref, ein_ref, eout_ref, o_ref,
+    am, ag, ym, zp, zfull, big, pp, sc, bo, bot, wg, acc, frecv, outg, es,
     z1, z2, z3, z4, p1, p2, p3, p4, w1, w2, w3, w4,
     lsem, gsem, bsem, tsem, osem,
     a_s, a_r, b_s, b_r, w_s, w_r, o_s, o_r,
@@ -213,7 +206,7 @@
         return pl.ds(0, n) if h is None else pl.ds(h * (n // 2), n // 2)
 
     def bo_chunk(k):
-        return pltpu.make_async_copy(bo_ref.at[wide(k)], bo.at[c, wide(k)], bsem.at[k])
+        return pltpu.make_async_copy(bo_ref.at[wide(k)], bo.at[wide(k)], bsem.at[k])
 
     def g_chunk(k):
         b = k % 4
@@ -221,10 +214,10 @@
 
     def bi_chunk(j):
         return pltpu.make_async_copy(
-            bi_ref.at[j, :, :, wide(rep)], big.at[j, :, at(m * 16, 16, 16)], tsem.at[j]
+            bi_ref.at[j, :, :, wide(rep)], big.at[:, at(j * 128 + m * 16, 16, 16)], tsem.at[j]
         )
 
-    load_a = pltpu.make_async_copy(at_ref, ag.at[:, x, yl], lsem.at[0])
+    load_a = pltpu.make_async_copy(a_ref, am, lsem.at[0])
     load_a.start()
     for k in range(4):
         bo_chunk(k).start()
@@ -236,38 +229,57 @@
 
     ga = Gather(lambda j, p, q, h: ag.at[j, q, p, halves(h, a_rows)], a_ways, a_s, a_r, yl, x, over_owner)
     gb = Gather(
-        lambda j, p, q, h: big.at[j, halves(h, 8), at((p * 4 + q) * 16, 16, 16)],
+        lambda j, p, q, h: big.at[halves(h, 8), at(j * 128 + (p * 4 + q) * 16, 16, 16)],
         b_ways, b_s, b_r, yl, x, over_owner,
     )
     gw = Gather(lambda j, p, q, h: wg.at[j, q * 2 + p, halves(h, p_rows)], g_ways, w_s, w_r, yh, z, over_dp)
     go = Gather(lambda j, p, q, h: outg.at[j, q * 2 + p, halves(h, o_rows)], o_ways, o_s, o_r, yh, z, over_dp)
-    rz = Reduce(a_parts, zp, (z1, z2, z3, z4), (zs, zr, zps, zpr), yh, z, over_dp)
-    rp = Reduce(p_parts, pp, (p1, p2, p3, p4), (ps, pr, pps, ppr), yh, z, over_dp)
-    rw = Reduce(p_parts, wp, (w1, w2, w3, w4), (xs, xr, xps, xpr), yl, x, over_owner)
+    rz = Reduce(zp, (z1, z2, z3, z4), (zs, zr, zps, zpr), yh, z, over_dp)
+    rp = Reduce(pp, (p1, p2, p3, p4), (ps, pr, pps, ppr), yh, z, over_dp)
+    rw = Reduce(pp, (w1, w2, w3, w4), (xs, xr, xps, xpr), yl, x, over_owner)
 
     half = pl.ds(0, 384)
     mine, other = at(c * 384, 384, 128), at(oc * 384, 384, 128)
-    send_bo = remote(bo_ref, bo.at[c], sib_s.at[0], sib_r.at[0], sibling)
+
+    def bot_copy(core):
+        ref = bot.at[at(core * 384, 384, 128)]
+        return remote(ref, ref, sib_s.at[0], sib_r.at[0], sibling)
+
     send_y = remote(ym.at[:, mine], ym.at[:, mine], sib_s.at[1], sib_r.at[1], sibling)
     send_f = remote(acc.at[:, other], frecv, sib_s.at[2], sib_r.at[2], sibling)
-    group = p_parts // b_parts
-    nt = (((1,), (1,)), ((), ()))
     tn = (((0,), (0,)), ((), ()))
+
+    lane = lax.broadcasted_iota(jnp.int32, (16, 128), 1)
+    place = lax.broadcasted_iota(jnp.int32, (16, 128), 0) + (z * 2 + yh) * 16
+
+    def eigen(_):
+        @pl.loop(0, 24)
+        def _(i):
+            row = ein_ref[pl.ds((2 * (i % 8) + c) * 3 + i // 8, 1), :]
+            column = jnp.sum(jnp.where(lane == place, row, 0.0), axis=1, keepdims=True)
+            es[at(i * 16, 16, 16), :] = jnp.broadcast_to(column, (16, 128))
 
     def y_step(k):
         bo_chunk(k).wait()
         g_chunk(k).wait()
         b = k % 4
         lhs = wg[:, pl.ds(2 * b, 2)].reshape(768, 768)
-        part = jnp.dot(lhs, bo[c, wide(k), :], preferred_element_type=f32)
+        part = jnp.dot(lhs, bo[wide(k), :], preferred_element_type=f32)
         acc[:, half] = part if k == 0 else acc[:, half] + part
         if k + 4 < 8:
             g_chunk(k + 4).start()
 
-    def y_out():
+    def y_out(_):
         ym[:, mine] = acc[:, half].astype(bf16)
         send_y.start()
-        send_bo.start()
+
+    def turn(k):
+        rows = pl.ds(k * 1536, 1536)
+        bot[mine, rows] = bo[rows, :].T
+        if k == 0:
+            eigen(k)
+        if k == 3:
+            bot_copy(c).start()
 
     def z_part(j):
         if j == 0:
@@ -288,42 +300,46 @@
         zfull[at(c * 384 + j * a_rows, a_rows, a_rows), :] = rz.result(j).astype(bf16)
         z_copy(j, c).start()
 
+    bi_seen = [0]
+
     def p_part(j):
         if j == 0:
             for i in range(a_parts):
                 z_copy(i, oc).wait_recv()
-        if j % group == 0:
-            gb.step("last", j // group)
-        rows = pl.ds((j % group) * p_rows, p_rows)
+        while bi_seen[0] * b_rows < (j + 1) * p_rows:
+            gb.step("last", bi_seen[0])
+            bi_seen[0] += 1
+        rows = pl.ds(j * p_rows, p_rows)
 
         @pl.loop(0, 2)
         def _(t):
-            lhs = big[j // group, pl.ds(4 * t, 4), rows, :].reshape(4 * p_rows, 768)
+            lhs = big[pl.ds(4 * t, 4), rows, :].reshape(4 * p_rows, 768)
             part = jnp.dot(lhs, zfull[...], preferred_element_type=f32)
             pp[j, pl.ds(2 * t, 2)] = part.astype(bf16).reshape(2, 2, p_rows, 768)
 
     def p_done(j):
-        scale = ein_ref[j] * eout_ref[pl.ds(m, 1), :] + damping
-        sc[j] = (rp.result(j) / scale).astype(bf16)
+        total = rp.result(j)
+        for b in range(6):
+            cols = slice(b * 128, (b + 1) * 128)
+            scale = es[pl.ds(j * p_rows, p_rows), :] * eout_ref[pl.ds(m * 6 + b, 1), :] + damping
+            sc[j, :, cols] = (total[:, cols] / scale).astype(bf16)
 
     def w_part(j):
         if j == 0:
-            remote(bo_ref, bo.at[oc], sib_s.at[0], sib_r.at[0], sibling).wait_recv()
+            bot_copy(oc).wait_recv()
+        rp.sent(j)
 
         @pl.loop(0, 8)
         def _(t):
-            rows = wide((t % 2) * 4 + t // 2)
-            part = lax.dot_general(sc[j, :, :384], bo[0, rows, :], nt, preferred_element_type=f32)
-            part += lax.dot_general(sc[j, :, 384:], bo[1, rows, :], nt, preferred_element_type=f32)
-            wp[j, t // 2, t % 2] = part.astype(bf16)
+            cols = wide((t % 2) * 4 + t // 2)
+            pp[j, t // 2, t % 2] = jnp.dot(sc[j], bot[:, cols], preferred_element_type=f32).astype(bf16)
 
     def w_done(j):
         wg[j, z * 2 + yh] = rw.result(j).astype(bf16)
 
     def out_part(j):
         gw.step("last", j)
-        rows = pl.ds((j % group) * p_rows, p_rows)
-        lhs = big[j // group, :, rows, :].reshape(8 * p_rows, 768)
+        lhs = big[:, pl.ds(j * p_rows, p_rows), :].reshape(8 * p_rows, 768)
         part = lax.dot_general(lhs, wg[j].reshape(8 * p_rows, 768), tn, preferred_element_type=f32)
         acc[...] = part if j == 0 else acc[...] + part
 
@@ -337,26 +353,28 @@
         rows = pl.ds(j * o_rows, o_rows)
         outg[j, z * 2 + yh] = (acc[rows, mine] + frecv[rows, :]).astype(bf16)
 
+    def f_out(_):
+        send_f.start()
+
     others = {
         "Zc": z_part, "Zr": z_done, "Pc": p_part, "Pr": p_done, "Wc": w_part, "Wr": w_done, "Oc": out_part,
-        "osum": out_sum, "Y": y_step,
+        "osum": out_sum, "T": turn, "Y": y_step, "yout": y_out, "fsend": f_out,
     }
     movers = {"A": ga, "B": gb, "G": gw, "O": go, "Z": rz, "P": rp, "W": rw}
 
     load_a.wait()
+    for t in range(3):
+        per = 128 // a_rows
+        ag[pl.ds(t * per, per), x, yl] = am[:, t * 128 : (t + 1) * 128].T.reshape(per, a_rows, 768)
     pl.semaphore_wait(barrier, len(partners))
     for step in order:
-        name = step.split(".")
-        if name[0] in others:
-            others[name[0]](int(name[1]))
-        elif name[0] in movers:
-            if name[0] == "B" and name[1] == "first":
-                bi_chunk(int(name[2])).wait()
-            movers[name[0]].step(name[1], int(name[2]))
-        elif step == "yout":
-            y_out()
+        name, j = steps[step // 16].split("."), step % 16
+        if len(name) == 1:
+            others[name[0]](j)
         else:
-            send_f.start()
+            if name == ["B", "first"]:
+                bi_chunk(j).wait()
+            movers[name[0]].step(name[1], j)
 
     for dp, dq in ((0, 0), (1, 0), (0, 1), (0, 3), (1, 1), (1, 3), (0, 2), (1, 2)):
         if (dp, dq) == (1, 0):
@@ -364,9 +382,13 @@
                 go.step("last", j)
         for j in range(o_parts):
             store(j, (yh + dp) % 2, (z + dq) % 4).start()
-    for mover in (ga, gb, gw, go, rz, rp, rw):
-        mover.sent()
-    for cp in (send_bo, send_y, send_f):
+    for gather in (ga, gb, gw, go):
+        gather.sent()
+    for j in range(a_parts):
+        rz.sent(j)
+    for j in range(p_parts):
+        rw.sent(j)
+    for cp in (bot_copy(c), send_y, send_f):
         cp.wait_send()
     for j in range(a_parts):
         z_copy(j, c).wait_send()
@@ -377,19 +399,14 @@
 
 
 def shards(activations, out_grads, basis_in, basis_out, eig_in, eig_out):
-    rep = lax.axis_index("dp")
-    core = lax.axis_index("owner") % 2
-    sub = (rep % 4) * 2 + rep // 4
-    ein = lax.dynamic_slice(eig_in.reshape(8, 2, 3, 8, 16), (0, core, 0, sub, 0), (8, 1, 3, 1, 16))
-    ein = ein.reshape(8, 3, 16).transpose(1, 0, 2).reshape(p_parts, p_rows, 1)
     dma = pltpu.SemaphoreType.DMA
     v = pltpu.VMEM
     scratch = [
-        v((a_parts, 4, 2, a_rows, 768), bf16), v((768, 768), bf16), v((a_parts, 4, 2, a_rows, 768), bf16),
-        v((768, 768), bf16), v((b_parts, 8, b_rows, 768), bf16), v((p_parts, 4, 2, p_rows, 768), bf16),
-        v((p_parts, p_rows, 768), bf16), v((2, 6144, 384), bf16), v((p_parts, 4, 2, p_rows, 768), bf16),
-        v((p_parts, 8, p_rows, 768), bf16), v((768, 768), f32), v((768, 384), f32),
-        v((o_parts, 8, o_rows, 384), bf16),
+        v((768, 384), bf16), v((a_parts, 4, 2, a_rows, 768), bf16), v((768, 768), bf16),
+        v((a_parts, 4, 2, a_rows, 768), bf16), v((768, 768), bf16), v((8, 384, 768), bf16),
+        v((p_parts, 4, 2, p_rows, 768), bf16), v((p_parts, p_rows, 768), bf16), v((6144, 384), bf16),
+        v((768, 6144), bf16), v((p_parts, 8, p_rows, 768), bf16), v((768, 768), f32), v((768, 384), f32),
+        v((o_parts, 8, o_rows, 384), bf16), v((384, 128), f32),
     ]
     for n, rows in ((a_parts, a_rows), (p_parts, p_rows), (p_parts, p_rows)):
         scratch += [
@@ -415,8 +432,8 @@
         ),
         name="precondition",
     )(
-        activations.T.reshape(a_parts, a_rows, 768), out_grads.reshape(p_parts, 2, p_rows, 6144),
-        basis_in.reshape(b_parts, 8, 16, 6144), basis_out, ein, eig_out.reshape(8, 768),
+        activations, out_grads.reshape(p_parts, 2, p_rows, 6144), basis_in.reshape(b_parts, 8, 16, 6144), basis_out,
+        eig_in.reshape(48, 128), eig_out.reshape(48, 128),
     )
 
 

time: 219 us -> 206 us (0.941)
  Pallas kernels: 208 us -> 201 us
  local copies, waits for them, and re-layouts: 10.1 us -> 4.99 us
    pallas_call x1, Pallas kernels: 208 us -> 201 us  [shards(): pl.pallas_call(kernel, out_shape=jax.ShapeDtypeStruct((6144, 384), bf16),...]
    reshape x3 -> x0, local copies, waits for them, and re-layouts: 2.99 us -> none  [the longest x1 1.34 us: shards(): eig_out.reshape(8, 768)]
where the time goes in v4:
time: 206 us
  Pallas kernels  201 us (98%)
  local copies, waits for them, and re-layouts  4.99 us (2%)
    pallas_call x1, Pallas kernels, shards(): pl.pallas_call(kernel, out_shape=jax.ShapeDtypeStruct((6144, 384), bf16),...  201 us
    unnamed x1, local copies, waits for them, and re-layouts  4.99 us

profile of v4, /device:TPU:1, one launch (start us, length us, event | category | flops | bytes accessed | tf_op | source)
XLA Modules:
  0.0 205.6 jit_solution(1838888040216773069)
XLA Ops:
  0.0 200.6 %precondition.1 = bf16[6144,384]{1,0:T(8,128)(2,1)} custom-call(bf16[768,384]{1,0:T(8,128)(2,1)} %a_ref.1, bf16[6,2,64,6144]{3,2,1,0:T(8,128)(2,1)} %bitcast.4, bf16[3,8,16,6144]{3,2,1,0:T(8,128)(2,1)} %bitcast.5, bf16[6144,384]{1,0:T(8,128)(2,1)} %bo_ref.1, f32[48,128]{1,0:T(8,128)} %bitcast.6, f32[48,128]{1,0:T(8,128)} %bitcast.7), custom_call_target="tpu_custom_call" | custom-call | tf_op jit(solution)/shard_map/precondition/pallas_call | solution.py:424
  200.7 5.0 %copy.8 = bf16[6144,384]{1,0:T(8,128)(2,1)} copy(bf16[6144,384]{1,0:T(8,128)(2,1)} %precondition.1) | data formatting | bytes 9437184

commit v5 on v4

v5 whole, which is shorter than its diff:
```python
import jax
import jax.numpy as jnp
from jax import lax
from jax.experimental import pallas as pl
from jax.experimental.pallas import tpu as pltpu
from jax.sharding import PartitionSpec as P

damping = 0.1
bf16 = jnp.bfloat16
f32 = jnp.float32
MESH = pl.DeviceIdType.MESH
a_parts, p_parts, b_parts, o_parts = 6, 6, 3, 6
a_rows, p_rows, b_rows, o_rows = 384 // a_parts, 384 // p_parts, 384 // b_parts, 768 // o_parts
a_ways, b_ways, g_ways, o_ways = 'yxyyxy', 'yyy', 'rrrrrr', 'yxyyxy'
steps = (
    "Y", "bar", "A.first", "A.f0", "A.f2", "A.f1", "yout", "T", "A.f4", "A.f3", "Zc", "Z.go", "Z.m0", "Z.m1",
    "Z.swap", "B.first", "Zr", "B.f2", "B.f1", "B.f0", "B.f3", "B.f4", "Pc", "P.go", "P.m1", "P.m0", "Pr", "Wc",
    "W.go", "W.m1", "W.m0", "W.swap", "Wr", "G.first", "G.f0", "G.f1", "Oc", "Ol", "osw", "osum", "O.first",
    "O.f2", "O.f1", "O.f0", "O.f4", "O.f3",
)
order = (
    0, 1, 2, 16, 32, 33, 3, 4, 5, 6, 7, 48, 64, 80, 96, 112, 81, 49, 113, 114, 128, 144, 34, 35, 65, 160, 176,
    66, 82, 50, 36, 67, 83, 51, 37, 192, 208, 161, 146, 130, 177, 84, 52, 224, 53, 193, 131, 147, 209, 69, 85,
    162, 68, 178, 225, 133, 149, 240, 241, 163, 179, 256, 210, 194, 165, 181, 211, 195, 272, 257, 288, 226, 273,
    304, 242, 289, 213, 197, 305, 227, 164, 180, 115, 320, 229, 258, 336, 290, 212, 196, 306, 274, 228, 259,
    337, 321, 261, 338, 260, 322, 352, 368, 353, 369, 355, 357, 384, 400, 371, 354, 385, 401, 370, 356, 372,
    416, 432, 448, 403, 387, 417, 402, 386, 433, 449, 388, 404, 464, 480, 419, 435, 451, 420, 436, 481, 465,
    418, 434, 483, 373, 496, 450, 467, 452, 497, 405, 389, 512, 528, 466, 421, 482, 437, 513, 529, 544, 453,
    499, 560, 468, 484, 561, 545, 498, 515, 531, 576, 469, 485, 577, 514, 530, 563, 547, 500, 501, 562, 546,
    516, 532, 517, 533, 578, 579, 548, 564, 549, 565, 580, 592, 593, 594, 595, 596, 597, 608, 609, 610, 611,
    612, 613, 624, 640, 625, 641, 626, 642, 656, 672, 627, 643, 689, 673, 628, 644, 674, 658, 629, 645, 675,
    659, 688, 657, 692, 676, 690, 677, 661, 691, 704, 720, 660, 722, 706, 693, 707, 723, 709, 725,
)


def device(yh, z, yl, x, c):
    return (yh * 4 + z, yl * 8 + x * 2 + c)


def remote(src, dst, s, r, dest):
    return pltpu.make_async_remote_copy(src, dst, s, r, device_id=dest, device_id_type=MESH)


class Gather:
    def __init__(self, part, ways, ssem, rsem, p, q, to):
        self.part, self.ways, self.ssem, self.rsem, self.p, self.q, self.to = part, ways, ssem, rsem, p, q, to

    def plan(self, j):
        p, q = self.p, self.q
        o, r, l, a = 1 - p, (q + 1) % 4, (q + 3) % 4, (q + 2) % 4
        if self.ways[j] == "r":
            return (
                ((p, q, None), (p, r), (p, l, None)),
                ((p, q, None), (p, l), (p, r, None)),
                ((p, l, 0), (p, r), (p, a, 0)),
                ((p, r, 1), (p, l), (p, a, 1)),
            )
        if self.ways[j] == "y":
            return (
                ((p, q, None), (o, q), (o, q, None)),
                ((p, q, None), (p, r), (p, l, None)),
                ((p, q, None), (p, l), (p, r, None)),
                ((o, q, None), (p, r), (o, l, None)),
                ((o, q, None), (p, l), (o, r, None)),
                ((p, l, 0), (p, r), (p, a, 0)),
                ((p, r, 1), (p, l), (p, a, 1)),
                ((o, l, 0), (p, r), (o, a, 0)),
                ((o, r, 1), (p, l), (o, a, 1)),
            )
        return (
            ((p, q, None), (p, r), (p, l, None)),
            ((p, q, None), (p, l), (p, r, None)),
            ((p, l, 0), (p, r), (p, a, 0)),
            ((p, r, 1), (p, l), (p, a, 1)),
            ((p, q, None), (o, q), (o, q, None)),
            ((p, l, None), (o, q), (o, l, None)),
            ((p, r, None), (o, q), (o, r, None)),
            ((p, a, None), (o, q), (o, a, None)),
        )

    def copy(self, j, k):
        block, dest, _ = self.plan(j)[k]
        ref = self.part(j, *block)
        return remote(ref, ref, self.ssem.at[j, k], self.rsem.at[j, k], self.to(*dest))

    def start(self, j, *ks):
        for k in ks:
            self.copy(j, k).start()

    def got(self, j, *ks):
        for k in ks:
            _, dest, block = self.plan(j)[k]
            ref = self.part(j, *block)
            remote(ref, ref, self.ssem.at[j, k], self.rsem.at[j, k], self.to(*dest)).wait_recv()

    def step(self, what, j):
        if self.ways[j] == "r":
            waits, starts = {
                "first": ((), (0, 1)),
                "f0": ((0,), (2,)),
                "f1": ((1,), (3,)),
                "last": ((2, 3), ()),
            }[what]
        elif self.ways[j] == "y":
            waits, starts = {
                "first": ((), (0, 1, 2)),
                "f0": ((0,), (3, 4)),
                "f1": ((1,), (5,)),
                "f2": ((2,), (6,)),
                "f3": ((3,), (7,)),
                "f4": ((4,), (8,)),
                "last": ((5, 6, 7, 8), ()),
            }[what]
        else:
            waits, starts = {
                "first": ((), (0, 1, 4)),
                "f0": ((0,), (2, 5)),
                "f1": ((1,), (3, 6)),
                "f2": ((2, 3), (7,)),
                "last": ((4, 5, 6, 7), ()),
            }[what]
        self.got(j, *waits)
        self.start(j, *starts)

    def sent(self):
        for j in range(len(self.ways)):
            for k in range(len(self.plan(j))):
                self.copy(j, k).wait_send()


class Reduce:
    def __init__(self, src, bufs, sems, p, q, to, how):
        self.src, self.p, self.q, self.to, self.how = src, p, q, to, how
        self.mid, self.end = bufs[:2]
        self.ssem, self.rsem = sems[:2]
        if how != "ring":
            self.out, self.got = bufs[2:]
            self.psem, self.qsem = sems[2:]

    def copy(self, j, k):
        q = self.q
        r, l, a = (q + 1) % 4, (q + 3) % 4, (q + 2) % 4
        right, left = self.to(self.p, r), self.to(self.p, l)
        src, dst, dest = (
            (self.src.at[j, a, 0], self.mid.at[j, 0], right),
            (self.src.at[j, a, 1], self.mid.at[j, 1], left),
            (self.src.at[j, r, 1], self.end.at[j, 0, 1], right),
            (self.src.at[j, l, 0], self.end.at[j, 1, 0], left),
            (self.src.at[j, r, 0], self.end.at[j, 0, 0], right),
            (self.src.at[j, l, 1], self.end.at[j, 1, 1], left),
        )[k]
        return remote(src, dst, self.ssem.at[j, k], self.rsem.at[j, k], dest)

    def pair(self, j):
        return remote(
            self.out.at[j], self.got.at[j], self.psem.at[j], self.qsem.at[j], self.to(1 - self.p, self.q)
        )

    def total(self, j, h):
        return (
            self.src[j, self.q, h].astype(f32) + self.end[j, 0, h].astype(f32) + self.end[j, 1, h].astype(f32)
        )

    def step(self, what, j):
        if what == "go":
            for k in range(4):
                self.copy(j, k).start()
        elif what == "swap":
            self.ends(j)
            if self.how == "both":
                for h in range(2):
                    self.out[j, h] = self.total(j, h).astype(bf16)
            else:
                self.out[j] = self.total(j, 1 - self.p).astype(bf16)
            self.pair(j).start()
        else:
            h = 0 if what == "m0" else 1
            t = (self.q + 1 + 2 * h) % 4
            self.copy(j, h).wait_recv()
            self.src[j, t, h] = self.src[j, t, h] + self.mid[j, h]
            self.copy(j, 4 + h).start()

    def ends(self, j):
        for k in range(2, 6):
            self.copy(j, k).wait_recv()

    def result(self, j):
        self.pair(j).wait_recv()
        if self.how == "both":
            return [self.total(j, h) + self.got[j, h].astype(f32) for h in range(2)]
        return self.total(j, self.p) + self.got[j].astype(f32)

    def sent(self, j):
        for k in range(6):
            self.copy(j, k).wait_send()
        if self.how != "ring":
            self.pair(j).wait_send()


def kernel(
    a_ref, g_ref, bi_ref, bo_ref, ein_ref, eout_ref, o_ref,
    am, ag, ym, zp, zfull, big, pp, sc, bo, bot, wg, acc, fs, fr, os, og, es,
    z1, z2, z3, z4, p1, p2, w1, w2, w3, w4,
    lsem, gsem, bsem, tsem,
    a_s, a_r, b_s, b_r, w_s, w_r, o_s, o_r,
    zs, zr, zps, zpr, ps, pr, xs, xr, xps, xpr, sib_s, sib_r, zsib_s, zsib_r, fsib_s, fsib_r, osw_s, osw_r,
):
    rep = lax.axis_index("dp")
    own = lax.axis_index("owner")
    yh, z = rep // 4, rep % 4
    yl, x, c = own // 8, (own // 2) % 4, own % 2
    m = yl * 4 + x
    oc = 1 - c

    sibling = device(yh, z, yl, x, oc)
    over_owner = lambda p, q: device(yh, z, p, q, c)
    over_dp = lambda p, q: device(p, q, yl, x, c)

    barrier = pltpu.get_barrier_semaphore()
    partners = [sibling, over_dp(1 - yh, z), over_owner(1 - yl, x)]
    partners += [over_owner(yl, (x + d) % 4) for d in (1, 3)]
    partners += [over_dp(yh, (z + d) % 4) for d in (1, 3)]
    for dest in partners:
        pl.semaphore_signal(barrier, inc=1, device_id=dest, device_id_type=MESH)

    def at(start, size, step):
        return pl.ds(pl.multiple_of(start, step), size)

    def wide(k):
        return at(k * 768, 768, 768)

    def halves(h, n):
        return pl.ds(0, n) if h is None else pl.ds(h * (n // 2), n // 2)

    def bo_chunk(k):
        return pltpu.make_async_copy(bo_ref.at[wide(k)], bo.at[wide(k)], bsem.at[k])

    def g_chunk(k):
        b = k % 4
        return pltpu.make_async_copy(g_ref.at[:, :, :, wide(k)], zp.at[:, b], gsem.at[b])

    def bi_chunk(j, h):
        dst = big.at[:, at(j * 128 + m * 16, 16, 16), pl.ds(h * 768, 768)]
        return pltpu.make_async_copy(bi_ref.at[j, :, yh, :, wide(h * 4 + z)], dst, tsem.at[j, h])

    load_a = pltpu.make_async_copy(a_ref, am, lsem.at[0])
    load_a.start()
    for k in range(4):
        bo_chunk(k).start()
        g_chunk(k).start()
    for k in range(4, 8):
        bo_chunk(k).start()
    for j in range(b_parts):
        for h in range(2):
            bi_chunk(j, h).start()

    ga = Gather(lambda j, p, q, h: ag.at[j, q, p, halves(h, a_rows)], a_ways, a_s, a_r, yl, x, over_owner)
    gb = Gather(
        lambda j, p, q, h: big.at[halves(h, 4), at(j * 128 + (p * 4 + q) * 16, 16, 16)],
        b_ways, b_s, b_r, yl, x, over_owner,
    )
    gw = Gather(lambda j, p, q, h: wg.at[j, q, halves(h, p_rows)], g_ways, w_s, w_r, yh, z, over_dp)
    go = Gather(lambda j, p, q, h: o_ref.at[p * 4 + q, j, halves(h, o_rows)], o_ways, o_s, o_r, yh, z, over_dp)
    rz = Reduce(zp, (z1, z2, z3, z4), (zs, zr, zps, zpr), yh, z, over_dp, "both")
    rp = Reduce(pp, (p1, p2), (ps, pr), yh, z, over_dp, "ring")
    rw = Reduce(zp, (w1, w2, w3, w4), (xs, xr, xps, xpr), yl, x, over_owner, "split")

    top, half = pl.ds(0, 768), pl.ds(0, 384)
    mine, other = at(c * 384, 384, 128), at(oc * 384, 384, 128)

    def bot_copy(core):
        ref = bot.at[at(core * 384, 384, 128)]
        return remote(ref, ref, sib_s.at[0], sib_r.at[0], sibling)

    send_y = remote(ym.at[:, mine], ym.at[:, mine], sib_s.at[1], sib_r.at[1], sibling)
    tn = (((0,), (0,)), ((), ()))

    lane = lax.broadcasted_iota(jnp.int32, (16, 128), 1)
    place = lax.broadcasted_iota(jnp.int32, (16, 128), 0) + (z * 2 + yh) * 16

    def eigen(_):
        @pl.loop(0, 24)
        def _(i):
            row = ein_ref[pl.ds((2 * (i % 8) + c) * 3 + i // 8, 1), :]
            column = jnp.sum(jnp.where(lane == place, row, 0.0), axis=1, keepdims=True)
            es[at(i * 16, 16, 16), :] = jnp.broadcast_to(column, (16, 128))

    def y_step(k):
        bo_chunk(k).wait()
        g_chunk(k).wait()
        b = k % 4
        lhs = zp[:, b].reshape(768, 768)
        part = jnp.dot(lhs, bo[wide(k), :], preferred_element_type=f32)
        acc[top, half] = part if k == 0 else acc[top, half] + part
        if k + 4 < 8:
            g_chunk(k + 4).start()

    def y_out(_):
        ym[:, mine] = acc[top, half].astype(bf16)
        send_y.start()

    def turn(k):
        rows = pl.ds(k * 1536, 1536)
        bot[mine, rows] = bo[rows, :].T
        if k == 0:
            eigen(k)
        if k == 3:
            bot_copy(c).start()

    def z_part(j):
        if j == 0:
            remote(ym.at[:, other], ym.at[:, other], sib_s.at[1], sib_r.at[1], sibling).wait_recv()
        ga.step("last", j)

        @pl.loop(0, 2)
        def _(t):
            two = pl.ds(2 * t, 2)
            part = jnp.dot(ag[j, two].reshape(4 * a_rows, 768), ym[...], preferred_element_type=f32)
            zp[j, two] = part.astype(bf16).reshape(2, 2, a_rows, 768)

    def z_copy(j, core):
        ref = zfull.at[:, at(core * 384 + j * a_rows, a_rows, a_rows)]
        return remote(ref, ref, zsib_s.at[j], zsib_r.at[j], sibling)

    def z_done(j):
        for h, total in enumerate(rz.result(j)):
            zfull[h, at(c * 384 + j * a_rows, a_rows, a_rows), :] = total.astype(bf16)
        z_copy(j, c).start()

    bi_seen = [0]

    def p_part(j):
        if j == 0:
            for i in range(a_parts):
                z_copy(i, oc).wait_recv()
        while bi_seen[0] * b_rows < (j + 1) * p_rows:
            gb.step("last", bi_seen[0])
            bi_seen[0] += 1
        rows = pl.ds(j * p_rows, p_rows)

        @pl.loop(0, 2)
        def _(t):
            lhs = big[pl.ds(2 * t, 2), rows, :].reshape(2 * p_rows, 1536)
            part = jnp.dot(lhs, zfull[...].reshape(1536, 768), preferred_element_type=f32)
            pp[j, pl.ds(2 * t, 2)] = part.astype(bf16).reshape(2, 2, p_rows // 2, 768)

    def p_done(j):
        rp.ends(j)
        for h in range(2):
            total = rp.total(j, h)
            n = p_rows // 2
            for b in range(6):
                cols = slice(b * 128, (b + 1) * 128)
                scale = es[pl.ds(j * p_rows + h * n, n), :] * eout_ref[pl.ds(m * 6 + b, 1), :] + damping
                sc[j, pl.ds(h * n, n), cols] = (total[:, cols] / scale).astype(bf16)

    def w_part(j):
        if j == 0:
            bot_copy(oc).wait_recv()
            for i in range(a_parts):
                rz.sent(i)

        @pl.loop(0, 8)
        def _(t):
            cols = wide((t % 2) * 4 + t // 2)
            zp[j, t // 2, t % 2] = jnp.dot(sc[j], bot[:, cols], preferred_element_type=f32).astype(bf16)

    def w_done(j):
        wg[j, z] = rw.result(j).astype(bf16)

    def out_part(j):
        gw.step("last", j)
        lhs = big[:, pl.ds(j * p_rows, p_rows), :].reshape(4 * p_rows, 1536)
        part = lax.dot_general(lhs, wg[j].reshape(4 * p_rows, 768), tn, preferred_element_type=f32)
        acc[...] = part if j == 0 else acc[...] + part

    def f_copy(i):
        return remote(fs.at[i], fr.at[i], fsib_s.at[i], fsib_r.at[i], sibling)

    def out_last(i):
        j = p_parts - 1
        if i == 0:
            gw.step("last", j)
        for h in range(2):
            cols = pl.ds(h * 768 + i * o_rows, o_rows)
            lhs = big[:, pl.ds(j * p_rows, p_rows), cols].reshape(4 * p_rows, o_rows)
            part = lax.dot_general(lhs, wg[j].reshape(4 * p_rows, 768), tn, preferred_element_type=f32)
            acc[cols, :] = acc[cols, :] + part
            fs[i, h] = acc[cols, other].astype(bf16)
        f_copy(i).start()

    def o_copy(i):
        return remote(os.at[i], og.at[i], osw_s.at[i], osw_r.at[i], over_dp(1 - yh, z))

    def out_half(i, h):
        return acc[at(h * 768 + i * o_rows, o_rows, o_rows), mine] + fr[i, h].astype(f32)

    def out_swap(i):
        f_copy(i).wait_recv()
        os[i] = out_half(i, 1 - yh).astype(bf16)
        o_copy(i).start()

    def out_sum(i):
        o_copy(i).wait_recv()
        o_ref[rep, i] = (out_half(i, yh) + og[i].astype(f32)).astype(bf16)

    def enter(_):
        load_a.wait()
        for t in range(3):
            per = 128 // a_rows
            ag[pl.ds(t * per, per), x, yl] = am[:, t * 128 : (t + 1) * 128].T.reshape(per, a_rows, 768)
        pl.semaphore_wait(barrier, len(partners))

    others = {
        "Zc": z_part, "Zr": z_done, "Pc": p_part, "Pr": p_done, "Wc": w_part, "Wr": w_done, "Oc": out_part,
        "osw": out_swap, "osum": out_sum, "T": turn, "Y": y_step, "yout": y_out, "bar": enter, "Ol": out_last,
    }
    movers = {"A": ga, "B": gb, "G": gw, "O": go, "Z": rz, "P": rp, "W": rw}

    for step in order:
        name, j = steps[step // 16].split("."), step % 16
        if len(name) == 1:
            others[name[0]](j)
        else:
            if name == ["B", "first"]:
                bi_chunk(j, 0).wait()
                bi_chunk(j, 1).wait()
            movers[name[0]].step(name[1], j)

    for j in range(o_parts):
        go.step("last", j)
    for gather in (ga, gb, gw, go):
        gather.sent()
    for j in range(p_parts):
        rp.sent(j)
        rw.sent(j)
    for i in range(o_parts):
        f_copy(i).wait_send()
        o_copy(i).wait_send()
    bot_copy(c).wait_send()
    send_y.wait_send()
    for j in range(a_parts):
        z_copy(j, c).wait_send()


def shards(activations, out_grads, basis_in, basis_out, eig_in, eig_out):
    dma = pltpu.SemaphoreType.DMA
    v = pltpu.VMEM
    scratch = [
        v((768, 384), bf16), v((a_parts, 4, 2, a_rows, 768), bf16), v((768, 768), bf16),
        v((a_parts, 4, 2, a_rows, 768), bf16), v((2, 768, 768), bf16), v((4, 384, 1536), bf16),
        v((p_parts, 4, 2, p_rows // 2, 768), bf16), v((p_parts, p_rows, 768), bf16), v((6144, 384), bf16),
        v((768, 6144), bf16), v((p_parts, 4, p_rows, 768), bf16), v((1536, 768), f32),
        v((o_parts, 2, o_rows, 384), bf16), v((o_parts, 2, o_rows, 384), bf16), v((o_parts, o_rows, 384), bf16),
        v((o_parts, o_rows, 384), bf16), v((384, 128), f32),
        v((a_parts, 2, a_rows, 768), bf16), v((a_parts, 2, 2, a_rows, 768), bf16),
        v((a_parts, 2, a_rows, 768), bf16), v((a_parts, 2, a_rows, 768), bf16),
        v((p_parts, 2, p_rows // 2, 768), bf16), v((p_parts, 2, 2, p_rows // 2, 768), bf16),
        v((p_parts, 2, p_rows, 768), bf16), v((p_parts, 2, 2, p_rows, 768), bf16), v((p_parts, p_rows, 768), bf16),
        v((p_parts, p_rows, 768), bf16),
    ]
    scratch += [dma((1,)), dma((4,)), dma((8,)), dma((b_parts, 2))]
    for n in (a_parts, b_parts, p_parts, o_parts):
        scratch += [dma((n, 9))] * 2
    scratch += [dma((a_parts, 6))] * 2 + [dma((a_parts,))] * 2 + [dma((p_parts, 6))] * 4 + [dma((p_parts,))] * 2
    scratch += [dma((2,))] * 2 + [dma((a_parts,))] * 2 + [dma((o_parts,))] * 4
    hbm = pl.BlockSpec(memory_space=pl.ANY)
    vmem = pl.BlockSpec(memory_space=pltpu.VMEM)
    out = pl.pallas_call(
        kernel,
        out_shape=pltpu.VMEM((8, o_parts, o_rows, 384), bf16),
        in_specs=[hbm, hbm, hbm, hbm, vmem, vmem],
        out_specs=vmem,
        scratch_shapes=scratch,
        compiler_params=pltpu.CompilerParams(
            collective_id=0, has_side_effects=True, vmem_limit_bytes=59 * 2**20
        ),
        name="precondition",
    )(
        activations, out_grads.reshape(p_parts, 2, p_rows, 6144), basis_in.reshape(b_parts, 4, 2, 16, 6144), basis_out,
        eig_in.reshape(48, 128), eig_out.reshape(48, 128),
    )
    return out.reshape(6144, 384)


def solution(mesh):
    in_specs = (P("dp", "owner"), P("dp", None), P("owner", None), P(None, "owner"), P(), P())
    out_specs = P(None, "owner")
    return jax.shard_map(shards, mesh=mesh, in_specs=in_specs, out_specs=out_specs, check_vma=False)
```

time: 206 us -> 196 us (0.951)
  Pallas kernels: 201 us -> 192 us
  local copies, waits for them, and re-layouts: 4.99 us -> 2.19 us
    pallas_call x1, Pallas kernels: 201 us -> 192 us  [shards(): pl.pallas_call(kernel, out_shape=pltpu.VMEM((8, o_parts, o_rows, 384), bf...]
    unnamed x1, local copies, waits for them, and re-layouts: 4.99 us -> 2.19 us
where the time goes in v5:
time: 196 us; the launch traced here: 194 us
  Pallas kernels  192 us (98%)
  local copies, waits for them, and re-layouts  2.19 us (1%)
    pallas_call x1, Pallas kernels, shards(): pl.pallas_call(kernel, out_shape=pltpu.VMEM((8, o_parts, o_rows, 384), bf...  192 us

profile of v5, /device:TPU:1, one launch (start us, length us, event | category | flops | bytes accessed | tf_op | source)
XLA Modules:
  0.0 194.2 jit_solution(14931407009149153590)
XLA Ops:
  0.0 192.0 %precondition.1 = bf16[8,6,128,384]{3,2,1,0:T(8,128)(2,1)S(1)} custom-call(bf16[768,384]{1,0:T(8,128)(2,1)} %a_ref.1, bf16[6,2,64,6144]{3,2,1,0:T(8,128)(2,1)} %bitcast.6, bf16[3,4,2,16,6144]{4,3,2,1,0:T(8,128)(2,1)} %bitcast.7, bf16[6144,384]{1,0:T(8,128)(2,1)} %bo_ref.1, f32[48,128]{1,0:T(8,128)} %bitcast.8, f32[48,128]{1,0:T(8,128)} %bitcast.9), custom_call_target="tpu_custom_call" | custom-call | tf_op jit(solution)/shard_map/precondition/pallas_call | solution.py:469
  192.0 2.2 %copy.8 = bf16[6144,384]{1,0:T(8,128)(2,1)} copy(bf16[6144,384]{1,0:T(8,128)(2,1)S(1)} %bitcast.5) | data formatting | bytes 9437184

commit v6 on v5

--- a/solution.py
+++ b/solution.py
@@ -11,25 +11,26 @@
 MESH = pl.DeviceIdType.MESH
 a_parts, p_parts, b_parts, o_parts = 6, 6, 3, 6
 a_rows, p_rows, b_rows, o_rows = 384 // a_parts, 384 // p_parts, 384 // b_parts, 768 // o_parts
-a_ways, b_ways, g_ways, o_ways = 'yxyyxy', 'yyy', 'rrrrrr', 'yxyyxy'
+a_ways, b_ways, g_ways, o_ways = 'xyyyyy', 'yyy', 'rrrrrr', 'yxyyxy'
 steps = (
-    "Y", "bar", "A.first", "A.f0", "A.f2", "A.f1", "yout", "T", "A.f4", "A.f3", "Zc", "Z.go", "Z.m0", "Z.m1",
-    "Z.swap", "B.first", "Zr", "B.f2", "B.f1", "B.f0", "B.f3", "B.f4", "Pc", "P.go", "P.m1", "P.m0", "Pr", "Wc",
-    "W.go", "W.m1", "W.m0", "W.swap", "Wr", "G.first", "G.f0", "G.f1", "Oc", "Ol", "osw", "osum", "O.first",
-    "O.f2", "O.f1", "O.f0", "O.f4", "O.f3",
+    "Y", "bar", "A.first", "A.f0", "A.f1", "A.f2", "yout", "T", "A.f4", "A.f3", "Zc", "Z.go", "Z.m0", "Z.m1",
+    "Z.swap", "B.first", "B.f0", "B.f2", "B.f1", "B.f4", "B.f3", "Zr", "Pc", "P.go", "P.m1", "P.m0", "Pr", "Wc",
+    "Wd", "We", "W.m1", "W.m0", "W.swap", "Wr", "G.first", "G.f1", "G.f0", "Oc", "Ol", "osw", "osum", "O.first",
+    "O.f0", "O.f1", "O.f2", "O.f4", "O.f3",
 )
 order = (
-    0, 1, 2, 16, 32, 33, 3, 4, 5, 6, 7, 48, 64, 80, 96, 112, 81, 49, 113, 114, 128, 144, 34, 35, 65, 160, 176,
-    66, 82, 50, 36, 67, 83, 51, 37, 192, 208, 161, 146, 130, 177, 84, 52, 224, 53, 193, 131, 147, 209, 69, 85,
-    162, 68, 178, 225, 133, 149, 240, 241, 163, 179, 256, 210, 194, 165, 181, 211, 195, 272, 257, 288, 226, 273,
-    304, 242, 289, 213, 197, 305, 227, 164, 180, 115, 320, 229, 258, 336, 290, 212, 196, 306, 274, 228, 259,
-    337, 321, 261, 338, 260, 322, 352, 368, 353, 369, 355, 357, 384, 400, 371, 354, 385, 401, 370, 356, 372,
-    416, 432, 448, 403, 387, 417, 402, 386, 433, 449, 388, 404, 464, 480, 419, 435, 451, 420, 436, 481, 465,
-    418, 434, 483, 373, 496, 450, 467, 452, 497, 405, 389, 512, 528, 466, 421, 482, 437, 513, 529, 544, 453,
-    499, 560, 468, 484, 561, 545, 498, 515, 531, 576, 469, 485, 577, 514, 530, 563, 547, 500, 501, 562, 546,
-    516, 532, 517, 533, 578, 579, 548, 564, 549, 565, 580, 592, 593, 594, 595, 596, 597, 608, 609, 610, 611,
-    612, 613, 624, 640, 625, 641, 626, 642, 656, 672, 627, 643, 689, 673, 628, 644, 674, 658, 629, 645, 675,
-    659, 688, 657, 692, 676, 690, 677, 661, 691, 704, 720, 660, 722, 706, 693, 707, 723, 709, 725,
+    0, 16, 32, 33, 1, 2, 3, 48, 64, 34, 4, 5, 6, 65, 49, 80, 35, 7, 81, 96, 112, 113, 114, 115, 129, 145, 50,
+    66, 36, 82, 160, 176, 51, 130, 146, 52, 67, 37, 192, 208, 161, 83, 177, 53, 131, 162, 178, 193, 209, 224,
+    147, 68, 69, 132, 210, 84, 194, 133, 148, 85, 149, 240, 241, 163, 179, 164, 226, 180, 225, 195, 211, 256,
+    196, 212, 257, 165, 272, 181, 289, 273, 227, 228, 197, 213, 229, 305, 321, 304, 339, 337, 338, 320, 340,
+    288, 242, 336, 341, 355, 371, 258, 274, 353, 369, 387, 290, 403, 352, 368, 401, 385, 354, 370, 306, 322,
+    419, 435, 451, 467, 400, 384, 417, 433, 449, 357, 373, 386, 402, 483, 416, 432, 499, 448, 389, 405, 356,
+    372, 497, 465, 481, 418, 434, 450, 515, 404, 480, 388, 496, 513, 420, 531, 436, 498, 482, 421, 437, 464,
+    547, 529, 545, 452, 484, 512, 466, 514, 500, 453, 469, 563, 577, 561, 485, 528, 544, 468, 501, 516, 530,
+    546, 576, 579, 560, 517, 532, 548, 562, 578, 533, 549, 592, 564, 593, 580, 594, 581, 565, 595, 596, 608,
+    609, 610, 611, 612, 624, 625, 613, 626, 627, 628, 629, 640, 656, 641, 657, 642, 658, 643, 659, 644, 660,
+    645, 661, 672, 689, 676, 688, 692, 673, 674, 675, 693, 706, 707, 722, 677, 723, 704, 708, 736, 691, 705,
+    738, 720, 739, 725, 690, 709, 741,
 )
 
 
@@ -163,8 +164,8 @@
 
     def step(self, what, j):
         if what == "go":
-            for k in range(4):
-                self.copy(j, k).start()
+            self.far(j)
+            self.near(j)
         elif what == "swap":
             self.ends(j)
             if self.how == "both":
@@ -180,6 +181,14 @@
             self.src[j, t, h] = self.src[j, t, h] + self.mid[j, h]
             self.copy(j, 4 + h).start()
 
+    def far(self, j):
+        self.copy(j, 0).start()
+        self.copy(j, 1).start()
+
+    def near(self, j):
+        self.copy(j, 2).start()
+        self.copy(j, 3).start()
+
     def ends(self, j):
         for k in range(2, 6):
             self.copy(j, k).wait_recv()
@@ -278,12 +287,19 @@
     lane = lax.broadcasted_iota(jnp.int32, (16, 128), 1)
     place = lax.broadcasted_iota(jnp.int32, (16, 128), 0) + (z * 2 + yh) * 16
 
-    def eigen(_):
+    def eigen():
         @pl.loop(0, 24)
         def _(i):
             row = ein_ref[pl.ds((2 * (i % 8) + c) * 3 + i // 8, 1), :]
             column = jnp.sum(jnp.where(lane == place, row, 0.0), axis=1, keepdims=True)
             es[at(i * 16, 16, 16), :] = jnp.broadcast_to(column, (16, 128))
+
+    done = set()
+
+    def once(name):
+        first = name not in done
+        done.add(name)
+        return first
 
     def y_step(k):
         bo_chunk(k).wait()
@@ -298,17 +314,16 @@
     def y_out(_):
         ym[:, mine] = acc[top, half].astype(bf16)
         send_y.start()
+        eigen()
 
     def turn(k):
         rows = pl.ds(k * 1536, 1536)
         bot[mine, rows] = bo[rows, :].T
-        if k == 0:
-            eigen(k)
         if k == 3:
             bot_copy(c).start()
 
     def z_part(j):
-        if j == 0:
+        if once("Z"):
             remote(ym.at[:, other], ym.at[:, other], sib_s.at[1], sib_r.at[1], sibling).wait_recv()
         ga.step("last", j)
 
@@ -330,7 +345,7 @@
     bi_seen = [0]
 
     def p_part(j):
-        if j == 0:
+        if once("P"):
             for i in range(a_parts):
                 z_copy(i, oc).wait_recv()
         while bi_seen[0] * b_rows < (j + 1) * p_rows:
@@ -355,15 +370,26 @@
                 sc[j, pl.ds(h * n, n), cols] = (total[:, cols] / scale).astype(bf16)
 
     def w_part(j):
-        if j == 0:
+        if once("W"):
             bot_copy(oc).wait_recv()
             for i in range(a_parts):
                 rz.sent(i)
 
-        @pl.loop(0, 8)
-        def _(t):
-            cols = wide((t % 2) * 4 + t // 2)
-            zp[j, t // 2, t % 2] = jnp.dot(sc[j], bot[:, cols], preferred_element_type=f32).astype(bf16)
+        w_block(j, (x + 2) % 4)
+        rw.far(j)
+
+    def w_block(j, t):
+        @pl.loop(0, 2)
+        def _(h):
+            zp[j, t, h] = jnp.dot(sc[j], bot[:, wide(h * 4 + t)], preferred_element_type=f32).astype(bf16)
+
+    def w_near(j):
+        w_block(j, (x + 1) % 4)
+        w_block(j, (x + 3) % 4)
+        rw.near(j)
+
+    def w_own(j):
+        w_block(j, x)
 
     def w_done(j):
         wg[j, z] = rw.result(j).astype(bf16)
@@ -412,7 +438,7 @@
         pl.semaphore_wait(barrier, len(partners))
 
     others = {
-        "Zc": z_part, "Zr": z_done, "Pc": p_part, "Pr": p_done, "Wc": w_part, "Wr": w_done, "Oc": out_part,
+        "Zc": z_part, "Zr": z_done, "Pc": p_part, "Pr": p_done, "Wc": w_part, "Wd": w_near, "We": w_own, "Wr": w_done, "Oc": out_part,
         "osw": out_swap, "osum": out_sum, "T": turn, "Y": y_step, "yout": y_out, "bar": enter, "Ol": out_last,
     }
     movers = {"A": ga, "B": gb, "G": gw, "O": go, "Z": rz, "P": rp, "W": rw}

time: 196 us -> 188 us (0.959)
  Pallas kernels: 192 us -> 185 us
    pallas_call x1, Pallas kernels: 192 us -> 185 us  [shards(): pl.pallas_call(kernel, out_shape=pltpu.VMEM((8, o_parts, o_rows, 384), bf...]
where the time goes in v6:
time: 188 us
  Pallas kernels  185 us (98%)
  local copies, waits for them, and re-layouts  2.19 us (1%)
    pallas_call x1, Pallas kernels, shards(): pl.pallas_call(kernel, out_shape=pltpu.VMEM((8, o_parts, o_rows, 384), bf...  185 us

profile of v6, /device:TPU:1, one launch (start us, length us, event | category | flops | bytes accessed | tf_op | source)
XLA Modules:
  0.0 187.6 jit_solution(18133243995444391850)
XLA Ops:
  0.0 185.4 %precondition.1 = bf16[8,6,128,384]{3,2,1,0:T(8,128)(2,1)S(1)} custom-call(bf16[768,384]{1,0:T(8,128)(2,1)} %a_ref.1, bf16[6,2,64,6144]{3,2,1,0:T(8,128)(2,1)} %bitcast.6, bf16[3,4,2,16,6144]{4,3,2,1,0:T(8,128)(2,1)} %bitcast.7, bf16[6144,384]{1,0:T(8,128)(2,1)} %bo_ref.1, f32[48,128]{1,0:T(8,128)} %bitcast.8, f32[48,128]{1,0:T(8,128)} %bitcast.9), custom_call_target="tpu_custom_call" | custom-call | tf_op jit(solution)/shard_map/precondition/pallas_call | solution.py:495
  185.4 2.2 %copy.8 = bf16[6144,384]{1,0:T(8,128)(2,1)} copy(bf16[6144,384]{1,0:T(8,128)(2,1)S(1)} %bitcast.5) | data formatting | bytes 9437184

commit v7 on v6

--- a/solution.py
+++ b/solution.py
@@ -13,24 +13,24 @@
 a_rows, p_rows, b_rows, o_rows = 384 // a_parts, 384 // p_parts, 384 // b_parts, 768 // o_parts
 a_ways, b_ways, g_ways, o_ways = 'xyyyyy', 'yyy', 'rrrrrr', 'yxyyxy'
 steps = (
-    "Y", "bar", "A.first", "A.f0", "A.f1", "A.f2", "yout", "T", "A.f4", "A.f3", "Zc", "Z.go", "Z.m0", "Z.m1",
-    "Z.swap", "B.first", "B.f0", "B.f2", "B.f1", "B.f4", "B.f3", "Zr", "Pc", "P.go", "P.m1", "P.m0", "Pr", "Wc",
-    "Wd", "We", "W.m1", "W.m0", "W.swap", "Wr", "G.first", "G.f1", "G.f0", "Oc", "Ol", "osw", "osum", "O.first",
-    "O.f0", "O.f1", "O.f2", "O.f4", "O.f3",
+    "Y", "bar", "A.first", "A.f0", "A.f1", "A.f2", "yout", "T", "A.f3", "A.f4", "Zc", "Z.go", "Z.m0", "Z.m1",
+    "Z.swap", "B.first", "Zr", "B.f0", "B.f1", "B.f2", "B.f3", "B.f4", "Pc", "P.go", "P.m1", "P.m0", "Pr", "Wc",
+    "Wd", "We", "W.m0", "W.m1", "W.swap", "Wr", "G.first", "G.f1", "G.f0", "Oc", "Ol", "osw", "osum", "O.first",
+    "O.f2", "O.f1", "O.f0", "O.f3", "O.f4",
 )
 order = (
-    0, 16, 32, 33, 1, 2, 3, 48, 64, 34, 4, 5, 6, 65, 49, 80, 35, 7, 81, 96, 112, 113, 114, 115, 129, 145, 50,
-    66, 36, 82, 160, 176, 51, 130, 146, 52, 67, 37, 192, 208, 161, 83, 177, 53, 131, 162, 178, 193, 209, 224,
-    147, 68, 69, 132, 210, 84, 194, 133, 148, 85, 149, 240, 241, 163, 179, 164, 226, 180, 225, 195, 211, 256,
-    196, 212, 257, 165, 272, 181, 289, 273, 227, 228, 197, 213, 229, 305, 321, 304, 339, 337, 338, 320, 340,
-    288, 242, 336, 341, 355, 371, 258, 274, 353, 369, 387, 290, 403, 352, 368, 401, 385, 354, 370, 306, 322,
-    419, 435, 451, 467, 400, 384, 417, 433, 449, 357, 373, 386, 402, 483, 416, 432, 499, 448, 389, 405, 356,
-    372, 497, 465, 481, 418, 434, 450, 515, 404, 480, 388, 496, 513, 420, 531, 436, 498, 482, 421, 437, 464,
-    547, 529, 545, 452, 484, 512, 466, 514, 500, 453, 469, 563, 577, 561, 485, 528, 544, 468, 501, 516, 530,
-    546, 576, 579, 560, 517, 532, 548, 562, 578, 533, 549, 592, 564, 593, 580, 594, 581, 565, 595, 596, 608,
-    609, 610, 611, 612, 624, 625, 613, 626, 627, 628, 629, 640, 656, 641, 657, 642, 658, 643, 659, 644, 660,
-    645, 661, 672, 689, 676, 688, 692, 673, 674, 675, 693, 706, 707, 722, 677, 723, 704, 708, 736, 691, 705,
-    738, 720, 739, 725, 690, 709, 741,
+    0, 16, 32, 33, 1, 2, 3, 4, 5, 48, 64, 49, 6, 7, 80, 34, 96, 112, 81, 129, 65, 145, 35, 160, 176, 50, 161,
+    51, 177, 82, 66, 36, 192, 146, 83, 130, 208, 113, 114, 115, 131, 147, 67, 209, 193, 52, 37, 224, 162, 178,
+    225, 53, 163, 179, 132, 84, 148, 68, 85, 69, 149, 133, 240, 241, 194, 210, 195, 211, 164, 180, 165, 181,
+    256, 272, 226, 196, 227, 212, 213, 289, 273, 305, 197, 228, 229, 320, 288, 337, 304, 259, 258, 336, 242,
+    260, 321, 261, 257, 352, 368, 274, 290, 353, 369, 354, 384, 400, 370, 355, 306, 371, 322, 338, 401, 385,
+    416, 432, 448, 387, 403, 402, 386, 417, 433, 449, 465, 357, 419, 435, 451, 480, 496, 356, 372, 464, 499,
+    373, 483, 418, 434, 512, 405, 497, 481, 388, 389, 404, 450, 498, 482, 466, 420, 436, 421, 513, 437, 467,
+    452, 515, 468, 484, 529, 500, 545, 453, 514, 469, 501, 485, 528, 544, 531, 547, 516, 560, 576, 530, 546,
+    517, 561, 577, 532, 548, 562, 578, 563, 533, 549, 592, 579, 593, 594, 580, 564, 581, 565, 595, 596, 608,
+    609, 610, 611, 624, 612, 613, 625, 626, 627, 628, 629, 640, 656, 641, 657, 642, 658, 672, 643, 659, 644,
+    660, 645, 661, 690, 704, 692, 689, 693, 677, 705, 674, 706, 708, 688, 720, 707, 673, 709, 736, 722, 739,
+    741, 723, 691, 738, 725, 675, 676,
 )
 
 

time: 188 us -> 188 us (level)
  no operation moved by 1% of the time
where the time goes in v7:
time: 188 us
  Pallas kernels  186 us (99%)
  local copies, waits for them, and re-layouts  2.19 us (1%)
    pallas_call x1, Pallas kernels, shards(): pl.pallas_call(kernel, out_shape=pltpu.VMEM((8, o_parts, o_rows, 384), bf...  186 us

profile of v7, /device:TPU:1, one launch (start us, length us, event | category | flops | bytes accessed | tf_op | source)
XLA Modules:
  0.0 187.8 jit_solution(16453093533097296346)
XLA Ops:
  0.0 185.6 %precondition.1 = bf16[8,6,128,384]{3,2,1,0:T(8,128)(2,1)S(1)} custom-call(bf16[768,384]{1,0:T(8,128)(2,1)} %a_ref.1, bf16[6,2,64,6144]{3,2,1,0:T(8,128)(2,1)} %bitcast.6, bf16[3,4,2,16,6144]{4,3,2,1,0:T(8,128)(2,1)} %bitcast.7, bf16[6144,384]{1,0:T(8,128)(2,1)} %bo_ref.1, f32[48,128]{1,0:T(8,128)} %bitcast.8, f32[48,128]{1,0:T(8,128)} %bitcast.9), custom_call_target="tpu_custom_call" | custom-call | tf_op jit(solution)/shard_map/precondition/pallas_call | solution.py:495
  185.6 2.2 %copy.8 = bf16[6144,384]{1,0:T(8,128)(2,1)} copy(bf16[6144,384]{1,0:T(8,128)(2,1)S(1)} %bitcast.5) | data formatting | bytes 9437184
